TPU v7x, 256 devices: a whole 4x4x8 slice. The times are simulated.
256 devices in a mesh: dp: 128 (over y, z, x), tensor: 2 (over core).
Axes of the slice: x: 4, y: 4, z: 8, core: 2. Of those that a mesh axis runs over, the one named last changes fastest.
Arguments:
- gradients: bfloat16 [128, 3, 768, 768], P('dp', None, None, 'tensor'), may hold values from -60 to 60
- error_feedback: float32 [128, 3, 768, 768], P('dp', None, None, 'tensor'), may hold values from -4 to 4
- warm_start: float32 [3, 768, 32], replicated, may hold values from -0.21875 to 0.21875
- weights: bfloat16 [3, 768, 768], P(None, None, 'tensor'), may hold values from -4 to 4
Outputs:
- next_error: float32 [128, 3, 768, 768], P('dp', None, None, 'tensor')
- new_weights: bfloat16 [3, 768, 768], P(None, None, 'tensor')
- right_factor: float32 [3, 768, 32], replicated
All inputs are finite; a program needn't handle non-finite values.
Results may differ from a plain program's by a relative error of at most 0.001.
Values sent between devices are 32-bit elements; how exact they have to be, the bound alone decides.
No kernel may reach another device: no remote copies, remote signals or barrier semaphores. Data moves between devices by JAX's collectives and lax.ppermute only.
A program may use at most 64 MiB of HBM per device.

v0:
```python
import jax
import jax.numpy as jnp
from jax import lax
from jax.sharding import PartitionSpec as P


def body(gradients, error_feedback, warm_start, weights):
    exact = lax.Precision.HIGHEST
    replicas_count = lax.axis_size("dp")
    merged = gradients.astype(jnp.float32) + error_feedback
    own_merged = merged[0]
    local_left = jnp.einsum("mrc,mrk->mck", own_merged, warm_start, precision=exact)
    left_full = lax.psum(local_left, "dp")
    gram_local = jnp.einsum("mck,mcl->mkl", left_full, left_full, precision=exact)
    gram_total = lax.psum(gram_local, "tensor")
    lower_factor = jnp.linalg.cholesky(gram_total)
    basis = lax.linalg.triangular_solve(
        lower_factor, left_full, left_side=False, lower=True, transpose_a=True
    )
    partial_right = jnp.einsum("mrc,mck->mrk", own_merged, basis, precision=exact)
    summed_right = lax.psum(partial_right, ("dp", "tensor"))
    right_factor = summed_right / replicas_count
    update = jnp.einsum("mrk,mck->mrc", right_factor, basis, precision=exact)
    next_error = merged - update[None]
    new_weights = (weights.astype(jnp.float32) - 0.5 * update).astype(jnp.bfloat16)
    return (next_error, new_weights, right_factor)


def solution(mesh):
    return jax.shard_map(
        body,
        mesh=mesh,
        in_specs=(
            P("dp", None, None, "tensor"),
            P("dp", None, None, "tensor"),
            P(),
            P(None, None, "tensor"),
        ),
        out_specs=(P("dp", None, None, "tensor"), P(None, None, "tensor"), P()),
        check_vma=False,
    )
```

profile of v0, /device:TPU:1, one launch (start us, length us, event | category | flops | bytes accessed | tf_op | source)
XLA Modules:
  0.0 514.8 jit_solution(1347558536988494906)
XLA Ops:
  7.2 0.0 copy-start
  7.2 0.0 copy-start.1
  7.2 0.0 all-reduce.3.cloned.1.call-start
  7.2 0.9 copy-done
  8.1 5.5 %fusion.2 = f32[3,384,32]{1,2,0:T(8,128)} fusion(f32[3,768,32]{1,2,0:T(8,128)S(1)} %copy-done, f32[1,3,768,384]{3,2,1,0:T(8,128)} %param.5, bf16[1,3,768,384]{3,2,1,0:T(8,128)(2,1)} %param.4), kind=kOutput, calls=%fused_computation.3 | convolution fusion | flops 341508096 | bytes 5750784 | tf_op jit(solution)/shard_map/mrc,mrk->mck/dot_general | solution.py:12
  13.6 0.0 all-reduce.3.cloned.1.call-update
  13.6 0.0 all-reduce.5.cloned.1.call-start
  13.7 211.0 %all-reduce.3.cloned.1.call-done = f32[3,384,32]{1,2,0:T(8,128)} async-done(((f32[3,384,32]{1,2,0:T(8,128)}), f32[3,384,32]{1,2,0:T(8,128)}) %all-reduce.3.cloned.1.call-update) | async-done | bytes 147472 | tf_op jit(solution)/shard_map/psum | solution.py:13
  224.7 1.3 fusion.7
  225.9 7.7 %psum.22 = f32[3,32,32]{1,2,0:T(8,128)S(1)} all-reduce(f32[3,32,32]{1,2,0:T(8,128)S(1)} %fusion.7), channel_id=1, replica_groups=mesh['dp'=128,'tensor'=2] {'tensor'}, use_global_device_ids=true, to_apply=%region_1.0 | all-reduce | flops 3072 | bytes 24576 | tf_op jit(solution)/shard_map/psum | solution.py:15
  233.7 0.1 copy.11
  233.8 8.8 %custom-call.7 = f32[3,32,32]{2,1,0:T(8,128)S(1)} custom-call(f32[3,32,32]{2,1,0:T(8,128)S(1)} %fusion.6), custom_call_target="Cholesky" | custom-call | tf_op jit(solution)/shard_map/jit(cholesky)/cholesky | solution.py:16
  242.6 0.1 compare_reduce_fusion
  242.7 0.1 select_bitcast_fusion
  242.8 7.4 %custom-call.8 = f32[3,1,32,32]{2,3,1,0:T(8,128)S(1)} custom-call(f32[3,1,32,32]{3,2,1,0:T(8,128)S(1)} %select_bitcast_fusion), custom_call_target="InvertDiagBlocksLowerTriangular" | custom-call | tf_op jit(solution)/shard_map/triangular_solve | solution.py:17
  250.2 1.3 fusion.4
  251.4 0.0 copy-done.1
  251.4 6.3 %fusion = f32[3,768,32]{1,2,0:T(8,128)} fusion(f32[3,384,32]{1,2,0:T(8,128)S(1)} %fusion.4, f32[1,3,768,384]{3,2,1,0:T(8,128)} %param.5, bf16[1,3,768,384]{3,2,1,0:T(8,128)(2,1)S(1)} %copy-done.1), kind=kOutput, calls=%fused_computation.1 | convolution fusion | flops 341508096 | bytes 5750784 | tf_op jit(solution)/shard_map/mrc,mck->mrk/dot_general | solution.py:20
  257.7 0.0 all-reduce.5.cloned.1.call-update
  257.8 241.5 %all-reduce.5.cloned.1.call-done = f32[3,768,32]{1,2,0:T(8,128)} async-done(((f32[3,768,32]{1,2,0:T(8,128)}), f32[3,768,32]{1,2,0:T(8,128)}) %all-reduce.5.cloned.1.call-update) | async-done | bytes 294928 | tf_op jit(solution)/shard_map/psum | solution.py:21
  499.2 1.0 broadcast_multiply_fusion
  500.2 0.0 copy-start.3
  500.2 0.0 copy-start.2
  500.2 6.1 %bitcast_subtract_fusion = (f32[1,3,768,384]{3,2,1,0:T(8,128)}, f32[3,768,384]{2,1,0:T(8,128)S(1)}) fusion(f32[1,3,768,384]{3,2,1,0:T(8,128)} %param.5, bf16[1,3,768,384]{3,2,1,0:T(8,128)(2,1)S(1)} %copy-done.1, f32[3,768,32]{1,2,0:T(8,128)S(1)} %broadcast_multiply_fusion, f32[3,384,32]{1,2,0:T(8,128)S(1)} %fusion.4), kind=kOutput, calls=%fused_computation | convolution fusion | flops 342392832 | bytes 12828672 | tf_op jit(solution)/shard_map/mrk,mck->mrc/dot_general | solution.py:23
  506.4 0.0 copy-done.3
  506.4 0.0 copy-done.2
  506.4 1.6 subtract_convert_fusion
  (4 shorter events, 0.1 us)
Async XLA Ops:
  7.2 1.0 copy-start
  7.2 244.2 %copy-start.1 = (bf16[1,3,768,384]{3,2,1,0:T(8,128)(2,1)S(1)}, bf16[1,3,768,384]{3,2,1,0:T(8,128)(2,1)}, u32[]{:S(2)}) copy-start(bf16[1,3,768,384]{3,2,1,0:T(8,128)(2,1)} %param.4) | copy-start | bytes 5308420
  7.2 217.5 %all-reduce.3.cloned.1.call-start = ((), (), s32[]{:S(2)}) async-start(), calls=%async_computation | async-start | bytes 294912 | tf_op jit(solution)/shard_map/psum | solution.py:13
  13.6 485.6 %all-reduce.5.cloned.1.call-start = ((), (), s32[]{:S(2)}) async-start(), calls=%async_computation.1 | async-start | bytes 589824 | tf_op jit(solution)/shard_map/psum | solution.py:21
  500.2 6.1 %copy-start.3 = (f32[3,768,32]{1,2,0:T(8,128)}, f32[3,768,32]{1,2,0:T(8,128)S(1)}, u32[]{:S(2)}) copy-start(f32[3,768,32]{1,2,0:T(8,128)S(1)} %broadcast_multiply_fusion) | copy-start | bytes 884740
  500.2 6.1 %copy-start.2 = (bf16[3,768,384]{2,1,0:T(8,128)(2,1)S(1)}, bf16[3,768,384]{2,1,0:T(8,128)(2,1)}, u32[]{:S(2)}) copy-start(bf16[3,768,384]{2,1,0:T(8,128)(2,1)} %param.7) | copy-start | bytes 5308420
Sparse Core Ops, SparseCore 0:
  14.1 210.5 all-reduce.2
  257.9 241.2 all-reduce.4
where the time goes:
time: 515 us
  waiting for transfers between devices  452 us (88%)
  matrix products  20.4 us (4%)
  other arithmetic  19 us (4%)
  between operations  14.1 us (3%)
  blocking collectives  7.72 us (1%)
    psum x1, waiting for transfers between devices, body(): summed_right = lax.psum(partial_right, ('dp', 'tensor'))  241 us
    psum x1, waiting for transfers between devices, body(): left_full = lax.psum(local_left, 'dp')  211 us
  transfers between devices with their start and end apart: 2, of which 2 were waited for; matrix products, arithmetic and copies ran while one was open for 0% of the time, Pallas kernels for 0%

commit v1 on v0

v1 whole, which is shorter than its diff:
```python
import jax
import jax.numpy as jnp
from jax import lax
from jax.experimental import pallas as pl
from jax.experimental.pallas import tpu as pltpu
from jax.sharding import PartitionSpec as P

Y, PLANE = 4, 32
PLANES = [[y * PLANE + i for i in range(PLANE)] for y in range(Y)]
PAIR = [(0, 1), (1, 0)]
MATS, ROWS, HALF, RANK = 3, 768, 384, 32
EXACT = lax.Precision.HIGHEST
PARAMS = pltpu.CompilerParams(vmem_limit_bytes=24 * 1024 * 1024)
WHOLE = pl.BlockSpec(memory_space=pltpu.VMEM)


def split(x):
    high = x.astype(jnp.bfloat16)
    rest = x - high.astype(jnp.float32)
    mid = rest.astype(jnp.bfloat16)
    low = (rest - mid.astype(jnp.float32)).astype(jnp.bfloat16)
    return high, mid, low


def stacked_dot(small, large, axis):
    stack = jnp.concatenate(split(small), axis=0)
    total = None
    for part in split(large):
        term = lax.dot_general(
            stack, part, (((1,), (axis,)), ((), ())), preferred_element_type=jnp.float32
        )
        total = term if total is None else total + term
    return total[:RANK] + (total[RANK : 2 * RANK] + total[2 * RANK :])


def left_kernel(g_ref, e_ref, w_ref, left_ref, merged_ref):
    m = pl.program_id(0)
    merged = g_ref[...].astype(jnp.float32) + e_ref[...]
    merged_ref[m] = merged
    left = stacked_dot(w_ref[...].T, merged, 0)
    for i in range(MATS):

        @pl.when(m == i)
        def _():
            left_ref[:, i, :] = left


def local_left(gradients, error_feedback, warm_start):
    return pl.pallas_call(
        left_kernel,
        grid=(MATS,),
        in_specs=[
            pl.BlockSpec((None, None, ROWS, HALF), lambda m: (0, m, 0, 0)),
            pl.BlockSpec((None, None, ROWS, HALF), lambda m: (0, m, 0, 0)),
            pl.BlockSpec((None, ROWS, RANK), lambda m: (m, 0, 0)),
        ],
        out_specs=[
            pl.BlockSpec((RANK, MATS, HALF), lambda m: (0, 0, 0)),
            WHOLE,
        ],
        out_shape=[
            jax.ShapeDtypeStruct((RANK, MATS, HALF), jnp.float32),
            pltpu.VMEM((MATS, ROWS, HALF), jnp.float32),
        ],
        compiler_params=PARAMS,
        name="local_left",
    )(gradients, error_feedback, warm_start)


def right_kernel(core_ref, merged_ref, left_ref, own_ref, other_ref):
    first = core_ref[0] == 0
    for m in range(MATS):
        left = left_ref[:, m, :]
        right = stacked_dot(left, merged_ref[m], 1)
        low, high = right[:, :HALF], right[:, HALF:]
        own_ref[:, m, :] = jnp.where(first, low, high)
        other_ref[:, m, :HALF] = jnp.where(first, high, low)
        gram = lax.dot_general(
            left,
            left,
            (((1,), (1,)), ((), ())),
            precision=EXACT,
            preferred_element_type=jnp.float32,
        )
        other_ref[:, m, HALF:] = jnp.concatenate(
            [gram, jnp.zeros((RANK, 128 - RANK), jnp.float32)], axis=1
        )


def local_right(core, merged, left):
    return pl.pallas_call(
        right_kernel,
        in_specs=[pl.BlockSpec(memory_space=pltpu.SMEM), WHOLE, WHOLE],
        out_specs=[WHOLE, WHOLE],
        out_shape=[
            jax.ShapeDtypeStruct((RANK, MATS, HALF), jnp.float32),
            jax.ShapeDtypeStruct((RANK, MATS, HALF + 128), jnp.float32),
        ],
        compiler_params=PARAMS,
        name="local_right",
    )(core, merged, left)


def inverse_kernel(mine_ref, theirs_ref, inverse_ref):
    row = lax.broadcasted_iota(jnp.int32, (RANK, 2 * RANK), 0)
    lane = lax.broadcasted_iota(jnp.int32, (RANK, 2 * RANK), 1)
    one = (lane == row + RANK).astype(jnp.float32)[:, RANK:]
    tables, pivots = [], []
    for m in range(MATS):
        gram = mine_ref[:, m, HALF:] + theirs_ref[:, m, HALF:]
        tables.append(jnp.concatenate([gram[:, :RANK], one], axis=1))
        pivots.append(jnp.zeros((RANK, 1), jnp.float32))
    for j in range(RANK):
        for m in range(MATS):
            table = tables[m]
            pivot = table[j : j + 1, j : j + 1]
            factor = jnp.where(row[:, :1] > j, table[:, j : j + 1], 0.0) / pivot
            pivots[m] = jnp.where(row[:, :1] == j, pivot, pivots[m])
            tables[m] = table - factor * table[j : j + 1, :]
    for m in range(MATS):
        inverse_ref[m] = tables[m][:, RANK:] * lax.rsqrt(pivots[m])


def inverse_factor(mine, theirs):
    return pl.pallas_call(
        inverse_kernel,
        in_specs=[WHOLE, WHOLE],
        out_specs=WHOLE,
        out_shape=jax.ShapeDtypeStruct((MATS, RANK, RANK), jnp.float32),
        compiler_params=PARAMS,
        name="inverse_factor",
    )(mine, theirs)


def final_kernel(
    replicas,
    core_ref,
    merged_ref,
    left_ref,
    own_ref,
    other_ref,
    inverse_ref,
    weights_ref,
    error_ref,
    new_ref,
    right_ref,
):
    first = core_ref[0] == 0
    m = pl.program_id(0)
    for i in range(MATS):

        @pl.when(m == i)
        def _():
            own, other = own_ref[:, i, :], other_ref[:, i, :]
            total = jnp.concatenate(
                [jnp.where(first, own, other), jnp.where(first, other, own)], axis=1
            )
            inverse = inverse_ref[i]
            right = jnp.dot(
                inverse, total, precision=EXACT, preferred_element_type=jnp.float32
            ) * (1.0 / replicas)
            basis = jnp.dot(
                inverse,
                left_ref[:, i, :],
                precision=EXACT,
                preferred_element_type=jnp.float32,
            )
            right_ref[...] = right.T
            rh, rm, _ = split(right)
            bh, bm, _ = split(basis)
            update = lax.dot_general(
                jnp.concatenate([rh, rh, rm], axis=0),
                jnp.concatenate([bh, bm, bh], axis=0),
                (((0,), (0,)), ((), ())),
                preferred_element_type=jnp.float32,
            )
            error_ref[...] = merged_ref[i] - update
            weights = weights_ref[...].astype(jnp.float32)
            new_ref[...] = (weights - 0.5 * update).astype(jnp.bfloat16)


def finish(core, merged, left, own, other, inverse, weights, replicas):
    def kernel(*refs):
        final_kernel(replicas, *refs)

    return pl.pallas_call(
        kernel,
        grid=(MATS,),
        in_specs=[
            pl.BlockSpec(memory_space=pltpu.SMEM),
            WHOLE,
            WHOLE,
            WHOLE,
            WHOLE,
            WHOLE,
            pl.BlockSpec((None, ROWS, HALF), lambda m: (m, 0, 0)),
        ],
        out_specs=[
            pl.BlockSpec((None, None, ROWS, HALF), lambda m: (0, m, 0, 0)),
            pl.BlockSpec((None, ROWS, HALF), lambda m: (m, 0, 0)),
            pl.BlockSpec((None, ROWS, RANK), lambda m: (m, 0, 0)),
        ],
        out_shape=[
            jax.ShapeDtypeStruct((1, MATS, ROWS, HALF), jnp.float32),
            jax.ShapeDtypeStruct((MATS, ROWS, HALF), jnp.bfloat16),
            jax.ShapeDtypeStruct((MATS, ROWS, RANK), jnp.float32),
        ],
        compiler_params=PARAMS,
        name="finish",
    )(core, merged, left, own, other, inverse, weights)


def exchange(blocks):
    return lax.all_to_all(
        blocks, "dp", 0, 0, axis_index_groups=PLANES, tiled=True
    )


def sum_over_replicas(blocks):
    part = jnp.sum(exchange(blocks), axis=0)
    met = {}
    for step in (2, 1, 3):
        partners = [
            (y * PLANE + i, (y ^ step) * PLANE + i)
            for y in range(Y)
            for i in range(PLANE)
        ]
        met[step] = lax.ppermute(part, "dp", partners)
    total = (part + met[1]) + (met[2] + met[3])
    return exchange(jnp.broadcast_to(total[None], blocks.shape))


def body(gradients, error_feedback, warm_start, weights):
    replicas = lax.axis_size("dp")
    core = lax.axis_index("tensor").astype(jnp.int32)[None]
    with jax.named_scope("left"):
        blocks, merged = local_left(gradients, error_feedback, warm_start)
    with jax.named_scope("sum_left"):
        left = sum_over_replicas(blocks)
    with jax.named_scope("right"):
        own, other = local_right(core, merged, left)
        received = lax.ppermute(other, "tensor", PAIR)
        inverse = inverse_factor(other, received)
    with jax.named_scope("sum_right"):
        own = sum_over_replicas(own + received[:, :, :HALF])
        other = lax.ppermute(own, "tensor", PAIR)
    with jax.named_scope("finish"):
        next_error, new_weights, right_factor = finish(
            core, merged, left, own, other, inverse, weights, replicas
        )
    return (next_error, new_weights, right_factor)


def solution(mesh):
    return jax.shard_map(
        body,
        mesh=mesh,
        in_specs=(
            P("dp", None, None, "tensor"),
            P("dp", None, None, "tensor"),
            P(),
            P(None, None, "tensor"),
        ),
        out_specs=(P("dp", None, None, "tensor"), P(None, None, "tensor"), P()),
        check_vma=False,
    )
```

time: 515 us -> 118 us (0.23)
  waiting for transfers between devices: 452 us -> 15.9 us
  blocking collectives: 7.72 us -> 49.7 us
  starting transfers between devices: 0.08 us -> 21.3 us
  matrix products: 20.4 us -> 0 us
  other arithmetic: 19 us -> 2.02 us
  local copies, waits for them, and re-layouts: 1 us -> 15.3 us
  between operations: 14.1 us -> 0.73 us
  Pallas kernels: 0 us -> 12.8 us
    psum x2 -> x0, waiting for transfers between devices: 452 us -> none  [the longest x1 241 us: body(): summed_right = lax.psum(partial_right, ('dp', 'tensor'))]
    all_to_all x0 -> x3, blocking collectives: none -> 49.7 us  [exchange(): lax.all_to_all(blocks, 'dp', 0, 0, axis_index_groups=PLANES, tiled=True)]
    dot_general x4 -> x0, matrix products: 19.2 us -> none  [the longest x1 6.31 us: body(): jnp.einsum('mrc,mck->mrk', own_merged, basis, precision=exact)]
    ppermute x0 -> x8, starting transfers between devices: none -> 16.6 us  [the longest x6 6.83 us: sum_over_replicas(): met[step] = lax.ppermute(part, 'dp', partners)]
    another operation x7 -> x0, other arithmetic: 16.4 us -> none  [the longest x4 8.96 us: body(): lower_factor = jnp.linalg.cholesky(gram_total)]
    pallas_call x0 -> x4, Pallas kernels: none -> 12.8 us  [the longest x1 4.56 us: finish(): pl.pallas_call(kernel, grid=(MATS,), in_specs=[pl.BlockSpec(memory_space=...]
    unnamed x8 -> x19, local copies, waits for them, and re-layouts: 0.92 us -> 12.2 us
    all_to_all x0 -> x1, waiting for transfers between devices: none -> 9.86 us  [exchange(): lax.all_to_all(blocks, 'dp', 0, 0, axis_index_groups=PLANES, tiled=True)]
  transfers between devices with their start and end apart: 2 -> 9, of which waited for: 2 -> 6; matrix products, arithmetic and copies ran while one was open for 0% -> 0% of each run, Pallas kernels for 0% -> 2%
where the time goes in v1:
time: 118 us
  blocking collectives  49.7 us (42%)
  starting transfers between devices  21.3 us (18%)
  waiting for transfers between devices  15.9 us (13%)
  local copies, waits for them, and re-layouts  15.3 us (13%)
  Pallas kernels  12.8 us (11%)
  other arithmetic  2.02 us (2%)
    all_to_all x3, blocking collectives, exchange(): lax.all_to_all(blocks, 'dp', 0, 0, axis_index_groups=PLANES, tiled=True)  49.7 us
    unnamed x19, local copies, waits for them, and re-layouts  12.2 us
    all_to_all x1, waiting for transfers between devices, exchange(): lax.all_to_all(blocks, 'dp', 0, 0, axis_index_groups=PLANES, tiled=True)  9.86 us
    ppermute x6, starting transfers between devices, sum_over_replicas(): met[step] = lax.ppermute(part, 'dp', partners)  6.83 us
    ppermute x1, starting transfers between devices, body(): received = lax.ppermute(other, 'tensor', PAIR)  5.37 us
    ppermute x6, waiting for transfers between devices, sum_over_replicas(): met[step] = lax.ppermute(part, 'dp', partners)  4.86 us
    all_to_all x1, starting transfers between devices, exchange(): lax.all_to_all(blocks, 'dp', 0, 0, axis_index_groups=PLANES, tiled=True)  4.71 us
    pallas_call x1, Pallas kernels, finish(): pl.pallas_call(kernel, grid=(MATS,), in_specs=[pl.BlockSpec(memory_space=...  4.56 us
  transfers between devices with their start and end apart: 9, of which 6 were waited for; matrix products, arithmetic and copies ran while one was open for 0% of the time, Pallas kernels for 2%

profile of v1, /device:TPU:1, one launch (start us, length us, event | category | flops | bytes accessed | tf_op | source)
XLA Modules:
  0.0 117.7 jit_solution(17649449168598150174)
XLA Ops:
  0.6 2.3 %copy.7.w_ref = f32[3,768,32]{2,1,0:T(8,128)} copy(f32[3,768,32]{1,2,0:T(8,128)} %param.6) | data formatting | bytes 589824 | tf_op args[2]
  3.0 1.3 %copy-done = f32[3,768,32]{2,1,0:T(8,128)S(1)} copy-done((f32[3,768,32]{2,1,0:T(8,128)S(1)}, f32[3,768,32]{2,1,0:T(8,128)}, u32[]{:S(2)}) %copy-start) | copy-done | bytes 294936
  4.3 2.0 %copy-done.1 = f32[1,3,768,384]{3,2,1,0:T(8,128)S(1)} copy-done((f32[1,3,768,384]{3,2,1,0:T(8,128)S(1)}, f32[1,3,768,384]{3,2,1,0:T(8,128)}, u32[]{:S(2)}) %copy-start.1) | copy-done | bytes 3538968
  6.3 1.5 %copy-done.2 = bf16[1,3,768,384]{3,2,1,0:T(8,128)(2,1)S(1)} copy-done((bf16[1,3,768,384]{3,2,1,0:T(8,128)(2,1)S(1)}, bf16[1,3,768,384]{3,2,1,0:T(8,128)(2,1)}, u32[]{:S(2)}) %copy-start.2) | copy-done | bytes 1769496
  7.7 1.8 %local_left.1 = (f32[32,3,384]{2,1,0:T(4,128)S(1)}, f32[3,768,384]{2,1,0:T(8,128)S(1)}) custom-call(bf16[1,3,768,384]{3,2,1,0:T(8,128)(2,1)S(1)} %copy-done.2, f32[1,3,768,384]{3,2,1,0:T(8,128)S(1)} %copy-done.1, f32[3,768,32]{2,1,0:T(8,128)S(1)} %copy-done), custom_call_target="tpu_custom_call" | custom-call | tf_op jit(solution)/shard_map/left/local_left/pallas_call | solution.py:49
  9.5 21.7 %all_to_all.20 = f32[32,3,384]{2,1,0:T(4,128)} all-to-all(f32[32,3,384]{2,1,0:T(4,128)S(1)} %get-tuple-element.8), channel_id=1, replica_groups={{0,2,4,6,8,10,12,14,16,18,20,22,24,26,28,30,32,34,36,38,40,42,44,46,48,..., dimensions={0} | all-to-all | bytes 294912 | tf_op jit(solution)/shard_map/sum_left/all_to_all | solution.py:214
  31.2 1.0 reduce_sum.18
  32.2 2.8 %collective-permute-start.2 = (f32[3,384]{1,0:T(4,128)S(1)}, f32[3,384]{1,0:T(4,128)S(1)}, u32[]{:S(2)}, u32[]{:S(2)}) collective-permute-start(f32[3,384]{1,0:T(4,128)S(1)} %reduce_sum.18), channel_id=1, source_target_pairs={{0,192},{2,194},{4,196},{6,198},{8,200},{10,202},{12,204},{14,206}... | collective-permute-start | bytes 13832 | tf_op jit(solution)/shard_map/sum_left/ppermute | solution.py:228
  36.1 3.0 %collective-permute-done.1 = f32[3,384]{1,0:T(4,128)S(1)} collective-permute-done((f32[3,384]{1,0:T(4,128)S(1)}, f32[3,384]{1,0:T(4,128)S(1)}, u32[]{:S(2)}, u32[]{:S(2)}) %collective-permute-start.1) | collective-permute-done | bytes 4640 | tf_op jit(solution)/shard_map/sum_left/ppermute | solution.py:228
  39.0 0.7 broadcast_in_dim.7
  39.7 4.7 %all-to-all-start.1 = ((f32[32,3,384]{2,1,0:T(4,128)}), f32[32,3,384]{2,1,0:T(4,128)}, u32[]{:S(2)}, u32[]{:S(2)}) async-start(f32[32,3,384]{2,1,0:T(4,128)} %broadcast_in_dim.7), calls=%async_computation.1 | async-start | bytes 393216 | tf_op jit(solution)/shard_map/sum_left/all_to_all | solution.py:214
  44.5 9.9 %all-to-all-done.1.left_ref.refs_2_ = f32[32,3,384]{2,1,0:T(4,128)} async-done(((f32[32,3,384]{2,1,0:T(4,128)}), f32[32,3,384]{2,1,0:T(4,128)}, u32[]{:S(2)}, u32[]{:S(2)}) %all-to-all-start.1) | async-done | bytes 147488 | tf_op jit(solution)/shard_map/sum_left/all_to_all | solution.py:214
  54.3 3.5 %local_right.1 = (f32[32,3,384]{2,1,0:T(4,128)S(1)}, f32[32,3,512]{2,1,0:T(4,128)S(1)}) custom-call(s32[1]{0:T(128)} %bitcast.core_ref.refs_0_, f32[3,768,384]{2,1,0:T(8,128)S(1)} %get-tuple-element.7.merged_ref.refs_1_, f32[32,3,384]{2,1,0:T(4,128)} %all-to-all-done.1.left_ref.refs_2_), custom_call_target="tpu_custom_call" | custom-call | tf_op jit(solution)/shard_map/right/local_right/pallas_call | solution.py:91
  57.9 5.4 %collective-permute-start.3 = (f32[32,3,512]{2,1,0:T(4,128)S(1)}, f32[32,3,512]{2,1,0:T(4,128)S(1)}, u32[]{:S(2)}, u32[]{:S(2)}) collective-permute-start(f32[32,3,512]{2,1,0:T(4,128)S(1)} %get-tuple-element.10.mine_ref), channel_id=1, source_target_pairs={{0,1},{1,0},{2,3},{3,2},{4,5},{5,4},{6,7},{7,6},{8,9},{9,8},{10,11... | collective-permute-start | bytes 589832 | tf_op jit(solution)/shard_map/right/ppermute | solution.py:242
  63.2 1.2 collective-permute-done.3.theirs_ref
  64.5 0.7 copy-done.5
  65.2 14.2 %all_to_all.21 = f32[32,3,384]{2,1,0:T(4,128)} all-to-all(f32[32,3,384]{2,1,0:T(4,128)S(1)} %slice_add_fusion), channel_id=1, replica_groups={{0,2,4,6,8,10,12,14,16,18,20,22,24,26,28,30,32,34,36,38,40,42,44,46,48,..., dimensions={0} | all-to-all | bytes 294912 | tf_op jit(solution)/shard_map/sum_right/all_to_all | solution.py:214
  79.3 1.0 reduce_sum.19
  80.3 0.9 collective-permute-start.6
  81.2 1.0 collective-permute-start.5
  82.2 1.4 %collective-permute-start.4 = (f32[3,384]{1,0:T(4,128)S(1)}, f32[3,384]{1,0:T(4,128)S(1)}, u32[]{:S(2)}, u32[]{:S(2)}) collective-permute-start(f32[3,384]{1,0:T(4,128)S(1)} %reduce_sum.19), channel_id=1, source_target_pairs={{0,64},{2,66},{4,68},{6,70},{8,72},{10,74},{12,76},{14,78},{16,80}... | collective-permute-start | bytes 13832 | tf_op jit(solution)/shard_map/sum_right/ppermute | solution.py:228
  83.6 0.4 collective-permute-done.6
  84.1 1.1 collective-permute-done.5
  85.2 13.9 %all_to_all.22.refs_3_ = f32[32,3,384]{2,1,0:T(4,128)S(1)} all-to-all(f32[32,3,384]{2,1,0:T(4,128)S(1)} %broadcast_in_dim.8), channel_id=1, replica_groups={{0,2,4,6,8,10,12,14,16,18,20,22,24,26,28,30,32,34,36,38,40,42,44,46,48,..., dimensions={0} | all-to-all | bytes 294912 | tf_op jit(solution)/shard_map/sum_right/all_to_all | solution.py:214
  99.1 4.4 %collective-permute-start.7 = (f32[32,3,384]{2,1,0:T(4,128)S(1)}, f32[32,3,384]{2,1,0:T(4,128)S(1)}, u32[]{:S(2)}, u32[]{:S(2)}) collective-permute-start(f32[32,3,384]{2,1,0:T(4,128)S(1)} %all_to_all.22.refs_3_), channel_id=1, source_target_pairs={{0,1},{1,0},{2,3},{3,2},{4,5},{5,4},{6,7},{7,6},{8,9},{9,8},{10,11... | collective-permute-start | bytes 442376 | tf_op jit(solution)/shard_map/sum_right/ppermute | solution.py:246
  103.5 0.9 copy-done.6
  104.4 0.9 copy-done.8
  105.4 2.9 %inverse_factor.1.refs_5_ = f32[3,32,32]{2,1,0:T(8,128)S(1)} custom-call(f32[32,3,512]{2,1,0:T(4,128)S(1)} %copy-done.8, f32[32,3,512]{2,1,0:T(4,128)S(1)} %copy-done.6), custom_call_target="tpu_custom_call" | custom-call | tf_op jit(solution)/shard_map/right/inverse_factor/pallas_call | solution.py:125
  108.3 1.5 %copy-done.3 = bf16[3,768,384]{2,1,0:T(8,128)(2,1)S(1)} copy-done((bf16[3,768,384]{2,1,0:T(8,128)(2,1)S(1)}, bf16[3,768,384]{2,1,0:T(8,128)(2,1)}, u32[]{:S(2)}) %copy-start.3) | copy-done | bytes 1769496
  109.7 4.6 %finish.1 = (f32[1,3,768,384]{3,2,1,0:T(8,128)}, bf16[3,768,384]{2,1,0:T(8,128)(2,1)}, f32[3,768,32]{2,1,0:T(8,128)S(1)}) custom-call(s32[1]{0:T(128)} %bitcast.core_ref.refs_0_, f32[3,768,384]{2,1,0:T(8,128)S(1)} %get-tuple-element.7.merged_ref.refs_1_, f32[32,3,384]{2,1,0:T(4,128)} %all-to-all-done.1.left_ref.refs_2_, ...), custom_call_target="tpu_custom_call" | custom-call | tf_op jit(solution)/shard_map/finish/finish/pallas_call | solution.py:186
  114.3 1.0 copy-done.4
  115.3 2.3 %copy.8 = f32[3,768,32]{1,2,0:T(8,128)} copy(f32[3,768,32]{2,1,0:T(8,128)} %copy-done.4) | data formatting | bytes 589824 | tf_op jit(solution)/shard_map/finish/finish/pallas_call | solution.py:186
  (20 shorter events, 1.1 us)
Async XLA Ops:
  3.0 1.3 %copy-start = (f32[3,768,32]{2,1,0:T(8,128)S(1)}, f32[3,768,32]{2,1,0:T(8,128)}, u32[]{:S(2)}) copy-start(f32[3,768,32]{2,1,0:T(8,128)} %copy.7.w_ref) | copy-start | bytes 884740
  4.2 2.0 %copy-start.1 = (f32[1,3,768,384]{3,2,1,0:T(8,128)S(1)}, f32[1,3,768,384]{3,2,1,0:T(8,128)}, u32[]{:S(2)}) copy-start(f32[1,3,768,384]{3,2,1,0:T(8,128)} %e_ref.1) | copy-start | bytes 10616836
  6.3 1.5 %copy-start.2 = (bf16[1,3,768,384]{3,2,1,0:T(8,128)(2,1)S(1)}, bf16[1,3,768,384]{3,2,1,0:T(8,128)(2,1)}, u32[]{:S(2)}) copy-start(bf16[1,3,768,384]{3,2,1,0:T(8,128)(2,1)} %g_ref.1) | copy-start | bytes 5308420
  32.2 3.8 %collective-permute-start.2 = (f32[3,384]{1,0:T(4,128)S(1)}, f32[3,384]{1,0:T(4,128)S(1)}, u32[]{:S(2)}, u32[]{:S(2)}) collective-permute-start(f32[3,384]{1,0:T(4,128)S(1)} %reduce_sum.18), channel_id=1, source_target_pairs={{0,192},{2,194},{4,196},{6,198},{8,200},{10,202},{12,204},{14,206}... | collective-permute-start | bytes 13832 | tf_op jit(solution)/shard_map/sum_left/ppermute | solution.py:228
  35.0 4.0 %collective-permute-start.1 = (f32[3,384]{1,0:T(4,128)S(1)}, f32[3,384]{1,0:T(4,128)S(1)}, u32[]{:S(2)}, u32[]{:S(2)}) collective-permute-start(f32[3,384]{1,0:T(4,128)S(1)} %reduce_sum.18), channel_id=1, source_target_pairs={{0,128},{2,130},{4,132},{6,134},{8,136},{10,138},{12,140},{14,142}... | collective-permute-start | bytes 13832 | tf_op jit(solution)/shard_map/sum_left/ppermute | solution.py:228
  35.4 3.6 %collective-permute-start = (f32[3,384]{1,0:T(4,128)S(1)}, f32[3,384]{1,0:T(4,128)S(1)}, u32[]{:S(2)}, u32[]{:S(2)}) collective-permute-start(f32[3,384]{1,0:T(4,128)S(1)} %reduce_sum.18), channel_id=1, source_target_pairs={{0,64},{2,66},{4,68},{6,70},{8,72},{10,74},{12,76},{14,78},{16,80}... | collective-permute-start | bytes 13832 | tf_op jit(solution)/shard_map/sum_left/ppermute | solution.py:228
  39.7 14.6 %all-to-all-start.1 = ((f32[32,3,384]{2,1,0:T(4,128)}), f32[32,3,384]{2,1,0:T(4,128)}, u32[]{:S(2)}, u32[]{:S(2)}) async-start(f32[32,3,384]{2,1,0:T(4,128)} %broadcast_in_dim.7), calls=%async_computation.1 | async-start | bytes 393216 | tf_op jit(solution)/shard_map/sum_left/all_to_all | solution.py:214
  57.8 6.6 %copy-start.7 = (f32[32,3,512]{2,1,0:T(4,128)}, f32[32,3,512]{2,1,0:T(4,128)S(1)}, u32[]{:S(2)}) copy-start(f32[32,3,512]{2,1,0:T(4,128)S(1)} %get-tuple-element.10.mine_ref) | copy-start | bytes 589828
  57.9 6.5 %collective-permute-start.3 = (f32[32,3,512]{2,1,0:T(4,128)S(1)}, f32[32,3,512]{2,1,0:T(4,128)S(1)}, u32[]{:S(2)}, u32[]{:S(2)}) collective-permute-start(f32[32,3,512]{2,1,0:T(4,128)S(1)} %get-tuple-element.10.mine_ref), channel_id=1, source_target_pairs={{0,1},{1,0},{2,3},{3,2},{4,5},{5,4},{6,7},{7,6},{8,9},{9,8},{10,11... | collective-permute-start | bytes 589832 | tf_op jit(solution)/shard_map/right/ppermute | solution.py:242
  64.5 0.7 copy-start.5
  80.3 3.8 %collective-permute-start.6 = (f32[3,384]{1,0:T(4,128)S(1)}, f32[3,384]{1,0:T(4,128)S(1)}, u32[]{:S(2)}, u32[]{:S(2)}) collective-permute-start(f32[3,384]{1,0:T(4,128)S(1)} %reduce_sum.19), channel_id=1, source_target_pairs={{0,192},{2,194},{4,196},{6,198},{8,200},{10,202},{12,204},{14,206}... | collective-permute-start | bytes 13832 | tf_op jit(solution)/shard_map/sum_right/ppermute | solution.py:228
  81.2 4.0 %collective-permute-start.5 = (f32[3,384]{1,0:T(4,128)S(1)}, f32[3,384]{1,0:T(4,128)S(1)}, u32[]{:S(2)}, u32[]{:S(2)}) collective-permute-start(f32[3,384]{1,0:T(4,128)S(1)} %reduce_sum.19), channel_id=1, source_target_pairs={{0,128},{2,130},{4,132},{6,134},{8,136},{10,138},{12,140},{14,142}... | collective-permute-start | bytes 13832 | tf_op jit(solution)/shard_map/sum_right/ppermute | solution.py:228
  82.2 3.0 %collective-permute-start.4 = (f32[3,384]{1,0:T(4,128)S(1)}, f32[3,384]{1,0:T(4,128)S(1)}, u32[]{:S(2)}, u32[]{:S(2)}) collective-permute-start(f32[3,384]{1,0:T(4,128)S(1)} %reduce_sum.19), channel_id=1, source_target_pairs={{0,64},{2,66},{4,68},{6,70},{8,72},{10,74},{12,76},{14,78},{16,80}... | collective-permute-start | bytes 13832 | tf_op jit(solution)/shard_map/sum_right/ppermute | solution.py:228
  99.1 9.1 %collective-permute-start.7 = (f32[32,3,384]{2,1,0:T(4,128)S(1)}, f32[32,3,384]{2,1,0:T(4,128)S(1)}, u32[]{:S(2)}, u32[]{:S(2)}) collective-permute-start(f32[32,3,384]{2,1,0:T(4,128)S(1)} %all_to_all.22.refs_3_), channel_id=1, source_target_pairs={{0,1},{1,0},{2,3},{3,2},{4,5},{5,4},{6,7},{7,6},{8,9},{9,8},{10,11... | collective-permute-start | bytes 442376 | tf_op jit(solution)/shard_map/sum_right/ppermute | solution.py:246
  103.5 0.9 copy-start.6
  104.4 0.9 copy-start.8
  108.3 1.5 %copy-start.3 = (bf16[3,768,384]{2,1,0:T(8,128)(2,1)S(1)}, bf16[3,768,384]{2,1,0:T(8,128)(2,1)}, u32[]{:S(2)}) copy-start(bf16[3,768,384]{2,1,0:T(8,128)(2,1)} %refs_6_.1) | copy-start | bytes 5308420
  114.3 1.0 copy-start.4

commit v2 on v1

v2 whole, which is shorter than its diff:
```python
import jax
import jax.numpy as jnp
from jax import lax
from jax.experimental import pallas as pl
from jax.experimental.pallas import tpu as pltpu
from jax.sharding import PartitionSpec as P

Y, PLANE = 4, 32
PLANES = [[y * PLANE + i for i in range(PLANE)] for y in range(Y)]
PAIR = [(0, 1), (1, 0)]
MATS, ROWS, HALF, RANK = 3, 768, 384, 32
EXACT = lax.Precision.HIGHEST
ORDER = (1, 2, 0)
CHUNK = 384
PARAMS = pltpu.CompilerParams(vmem_limit_bytes=24 * 1024 * 1024)
WHOLE = pl.BlockSpec(memory_space=pltpu.VMEM)


def in_hbm(x):
    return pltpu.with_memory_space_constraint(x, pltpu.HBM)


def split(x):
    high = x.astype(jnp.bfloat16)
    rest = x - high.astype(jnp.float32)
    mid = rest.astype(jnp.bfloat16)
    low = (rest - mid.astype(jnp.float32)).astype(jnp.bfloat16)
    return high, mid, low


def stacked_dot(small, large, axis):
    stack = jnp.concatenate(split(small), axis=0)
    total = None
    for part in split(large):
        term = lax.dot_general(
            stack, part, (((1,), (axis,)), ((), ())), preferred_element_type=jnp.float32
        )
        total = term if total is None else total + term
    return total[:RANK] + (total[RANK : 2 * RANK] + total[2 * RANK :])


def left_kernel(g_ref, e_ref, w_ref, left_ref, kept_ref, stored_ref, buffer, sem):
    m = pl.program_id(0)
    merged = g_ref[...].astype(jnp.float32) + e_ref[...]
    left = stacked_dot(w_ref[...], merged, 0)
    store = pltpu.make_async_copy(buffer, stored_ref, sem)
    for i in range(MATS):

        @pl.when(m == i)
        def _():
            left_ref[:, i, :] = left
            if i == 0:
                buffer[...] = merged
                store.start()
            else:
                kept_ref[i - 1] = merged
            if i == MATS - 1:
                store.wait()


def local_left(gradients, error_feedback, warm_rows):
    return pl.pallas_call(
        left_kernel,
        grid=(MATS,),
        in_specs=[
            pl.BlockSpec((None, None, ROWS, HALF), lambda m: (0, m, 0, 0)),
            pl.BlockSpec((None, None, ROWS, HALF), lambda m: (0, m, 0, 0)),
            pl.BlockSpec((None, RANK, ROWS), lambda m: (m, 0, 0)),
        ],
        out_specs=[
            pl.BlockSpec((RANK, MATS, HALF), lambda m: (0, 0, 0)),
            WHOLE,
            pl.BlockSpec(memory_space=pl.ANY),
        ],
        out_shape=[
            jax.ShapeDtypeStruct((RANK, MATS, HALF), jnp.float32),
            pltpu.VMEM((MATS - 1, ROWS, HALF), jnp.float32),
            pltpu.HBM((ROWS, HALF), jnp.float32),
        ],
        scratch_shapes=[
            pltpu.VMEM((ROWS, HALF), jnp.float32),
            pltpu.SemaphoreType.DMA,
        ],
        compiler_params=PARAMS,
        name="local_left",
    )(in_hbm(gradients), in_hbm(error_feedback), warm_rows)


def right_kernel(
    core_ref, kept_ref, stored_ref, left_ref, own_ref, other_ref, gram_ref, buffer, sem
):
    first = core_ref[0] == 0
    load = pltpu.make_async_copy(stored_ref, buffer, sem)
    load.start()
    for m in ORDER:
        left = left_ref[:, m, :]
        gram = lax.dot_general(
            left,
            left,
            (((1,), (1,)), ((), ())),
            precision=EXACT,
            preferred_element_type=jnp.float32,
        )
        gram = jnp.concatenate(
            [gram, jnp.zeros((RANK, 128 - RANK), jnp.float32)], axis=1
        )
        gram_ref[:, m, :] = gram
        other_ref[:, m, HALF:] = gram
        if m == 0:
            load.wait()
            merged = buffer[...]
        else:
            merged = kept_ref[m - 1]
        right = stacked_dot(left, merged, 1)
        low, high = right[:, :HALF], right[:, HALF:]
        own_ref[:, m, :] = jnp.where(first, low, high)
        other_ref[:, m, :HALF] = jnp.where(first, high, low)


def local_right(core, kept, stored, left):
    return pl.pallas_call(
        right_kernel,
        in_specs=[
            pl.BlockSpec(memory_space=pltpu.SMEM),
            WHOLE,
            pl.BlockSpec(memory_space=pl.ANY),
            WHOLE,
        ],
        out_specs=[WHOLE] * 3,
        out_shape=[
            jax.ShapeDtypeStruct((RANK, MATS, HALF), jnp.float32),
            jax.ShapeDtypeStruct((RANK, MATS, HALF + 128), jnp.float32),
            jax.ShapeDtypeStruct((RANK, MATS, 128), jnp.float32),
        ],
        scratch_shapes=[
            pltpu.VMEM((ROWS, HALF), jnp.float32),
            pltpu.SemaphoreType.DMA,
        ],
        compiler_params=PARAMS,
        name="local_right",
    )(core, kept, in_hbm(stored), left)


def inverse_kernel(gram_ref, inverse_ref):
    row = lax.broadcasted_iota(jnp.int32, (RANK, 2 * RANK), 0)
    lane = lax.broadcasted_iota(jnp.int32, (RANK, 2 * RANK), 1)
    one = (lane == row + RANK).astype(jnp.float32)[:, RANK:]
    tables, pivots = [], []
    for m in range(MATS):
        tables.append(jnp.concatenate([gram_ref[:, m, :RANK], one], axis=1))
        pivots.append(jnp.zeros((RANK, 1), jnp.float32))
    for j in range(RANK):
        for m in range(MATS):
            table = tables[m]
            pivot = table[j : j + 1, j : j + 1]
            factor = jnp.where(row[:, :1] > j, table[:, j : j + 1], 0.0) / pivot
            pivots[m] = jnp.where(row[:, :1] == j, pivot, pivots[m])
            tables[m] = table - factor * table[j : j + 1, :]
    for m in range(MATS):
        inverse_ref[m] = tables[m][:, RANK:] * lax.rsqrt(pivots[m])


def inverse_factor(gram):
    return pl.pallas_call(
        inverse_kernel,
        in_specs=[WHOLE],
        out_specs=WHOLE,
        out_shape=jax.ShapeDtypeStruct((MATS, RANK, RANK), jnp.float32),
        compiler_params=PARAMS,
        cost_estimate=pl.CostEstimate(
            flops=4_000_000, bytes_accessed=100_000, transcendentals=0
        ),
        name="inverse_factor",
    )(gram)


def finish_kernel(
    replicas,
    core_ref,
    kept_ref,
    stored_ref,
    left_ref,
    own_ref,
    other_ref,
    inverse_ref,
    weights_ref,
    error_ref,
    new_ref,
    right_ref,
    buffer,
    right_parts,
    basis_parts,
    sem,
):
    first = core_ref[0] == 0
    p, c = pl.program_id(0), pl.program_id(1)
    load = pltpu.make_async_copy(stored_ref, buffer, sem)
    rows = pl.ds(pl.multiple_of(c * CHUNK, CHUNK), CHUNK)

    @pl.when((p == 0) & (c == 0))
    def _():
        load.start()

    for i, m in enumerate(ORDER):

        @pl.when((p == i) & (c == 0))
        def _():
            own, other = own_ref[:, m, :], other_ref[:, m, :]
            total = jnp.concatenate(
                [jnp.where(first, own, other), jnp.where(first, other, own)], axis=1
            )
            inverse = inverse_ref[m]
            right = jnp.dot(
                inverse, total, precision=EXACT, preferred_element_type=jnp.float32
            ) * (1.0 / replicas)
            basis = jnp.dot(
                inverse,
                left_ref[:, m, :],
                precision=EXACT,
                preferred_element_type=jnp.float32,
            )
            right_ref[...] = right
            high, mid, _ = split(right)
            right_parts[...] = jnp.concatenate([high, high, mid], axis=0)
            high, mid, _ = split(basis)
            basis_parts[...] = jnp.concatenate([high, mid, high], axis=0)
            if m == 0:
                load.wait()

    update = lax.dot_general(
        right_parts[:, rows],
        basis_parts[...],
        (((0,), (0,)), ((), ())),
        preferred_element_type=jnp.float32,
    )
    weights = weights_ref[...].astype(jnp.float32)
    new_ref[...] = (weights - 0.5 * update).astype(jnp.bfloat16)
    for i, m in enumerate(ORDER):

        @pl.when(p == i)
        def _():
            merged = buffer[rows, :] if m == 0 else kept_ref[m - 1, rows, :]
            error_ref[...] = merged - update


def finish(core, kept, stored, left, own, other, inverse, weights, replicas):
    def kernel(*refs):
        finish_kernel(replicas, *refs)

    def at(p, c):
        return (lax.rem(p + 1, MATS), c, 0)

    return pl.pallas_call(
        kernel,
        grid=(MATS, ROWS // CHUNK),
        in_specs=[
            pl.BlockSpec(memory_space=pltpu.SMEM),
            WHOLE,
            pl.BlockSpec(memory_space=pl.ANY),
            WHOLE,
            WHOLE,
            WHOLE,
            WHOLE,
            pl.BlockSpec((None, CHUNK, HALF), at),
        ],
        out_specs=[
            pl.BlockSpec((None, None, CHUNK, HALF), lambda p, c: (0, *at(p, c))),
            pl.BlockSpec((None, CHUNK, HALF), at),
            pl.BlockSpec((None, RANK, ROWS), lambda p, c: (at(p, c)[0], 0, 0)),
        ],
        out_shape=[
            jax.ShapeDtypeStruct((1, MATS, ROWS, HALF), jnp.float32),
            jax.ShapeDtypeStruct((MATS, ROWS, HALF), jnp.bfloat16),
            jax.ShapeDtypeStruct((MATS, RANK, ROWS), jnp.float32),
        ],
        scratch_shapes=[
            pltpu.VMEM((ROWS, HALF), jnp.float32),
            pltpu.VMEM((3 * RANK, ROWS), jnp.bfloat16),
            pltpu.VMEM((3 * RANK, HALF), jnp.bfloat16),
            pltpu.SemaphoreType.DMA,
        ],
        compiler_params=PARAMS,
        name="finish",
    )(core, kept, in_hbm(stored), left, own, other, inverse, in_hbm(weights))


def exchange(blocks):
    return lax.all_to_all(
        blocks, "dp", 0, 0, axis_index_groups=PLANES, tiled=True
    )


def sum_over_replicas(blocks, beside=None):
    part = jnp.sum(exchange(blocks), axis=0)
    result = None
    if beside is not None:
        work, value = beside
        part, value = lax.optimization_barrier((part, value))
    met = {}
    for step in (2, 1, 3):
        partners = [
            (y * PLANE + i, (y ^ step) * PLANE + i)
            for y in range(Y)
            for i in range(PLANE)
        ]
        met[step] = lax.ppermute(part, "dp", partners)
    if beside is not None:
        result = work(value)
        met[1], met[2], met[3], result = lax.optimization_barrier(
            (met[1], met[2], met[3], result)
        )
    total = (part + met[1]) + (met[2] + met[3])
    return exchange(jnp.broadcast_to(total[None], blocks.shape)), result


def body(gradients, error_feedback, warm_start, weights):
    replicas = lax.axis_size("dp")
    core = lax.axis_index("tensor").astype(jnp.int32)[None]
    with jax.named_scope("left"):
        blocks, kept, stored = local_left(
            gradients, error_feedback, jnp.swapaxes(warm_start, 1, 2)
        )
    with jax.named_scope("sum_left"):
        left, _ = sum_over_replicas(blocks)
    with jax.named_scope("right"):
        own, other, gram = local_right(core, kept, stored, left)
        received = lax.ppermute(other, "tensor", PAIR)
        gram = gram + received[:, :, HALF:]
    with jax.named_scope("sum_right"):
        own, inverse = sum_over_replicas(
            own + received[:, :, :HALF], (inverse_factor, gram)
        )
        other = lax.ppermute(own, "tensor", PAIR)
    with jax.named_scope("finish"):
        next_error, new_weights, right_rows = finish(
            core, kept, stored, left, own, other, inverse, weights, replicas
        )
    return (next_error, new_weights, jnp.swapaxes(right_rows, 1, 2))


def solution(mesh):
    return jax.shard_map(
        body,
        mesh=mesh,
        in_specs=(
            P("dp", None, None, "tensor"),
            P("dp", None, None, "tensor"),
            P(),
            P(None, None, "tensor"),
        ),
        out_specs=(P("dp", None, None, "tensor"), P(None, None, "tensor"), P()),
        check_vma=False,
    )
```

time: 118 us -> 107 us (0.907)
  blocking collectives: 49.7 us -> 35.5 us
  local copies, waits for them, and re-layouts: 15.3 us -> 1.69 us
  waiting for transfers between devices: 15.9 us -> 26 us
  Pallas kernels: 12.8 us -> 18.4 us
  starting transfers between devices: 21.3 us -> 23.7 us
    all_to_all x3 -> x2, blocking collectives: 49.7 us -> 35.5 us  [exchange(): lax.all_to_all(blocks, 'dp', 0, 0, axis_index_groups=PLANES, tiled=True)]
    unnamed x19 -> x2, local copies, waits for them, and re-layouts: 12.2 us -> 0.95 us
    all_to_all x1 -> x2, waiting for transfers between devices: 9.86 us -> 20.4 us  [exchange(): lax.all_to_all(blocks, 'dp', 0, 0, axis_index_groups=PLANES, tiled=True)]
    all_to_all x1 -> x2, starting transfers between devices: 4.71 us -> 8.47 us  [exchange(): lax.all_to_all(blocks, 'dp', 0, 0, axis_index_groups=PLANES, tiled=True)]
    pallas_call x1, Pallas kernels: 1.81 us -> 4.65 us  [local_left(): pl.pallas_call(left_kernel, grid=(MATS,), in_specs=[pl.BlockSpec((None, N...]
    pallas_call x1 -> x0, local copies, waits for them, and re-layouts: 2.33 us -> none  [finish(): pl.pallas_call(kernel, grid=(MATS,), in_specs=[pl.BlockSpec(memory_space=...]
    pallas_call x2, Pallas kernels: 7.44 us -> 9.66 us  [the longest x1 6.79 us: finish(): pl.pallas_call(kernel, grid=(MATS, ROWS // CHUNK), in_specs=[pl.BlockSpec...]
    reduce_sum x2, other arithmetic: 1.95 us -> 0.11 us  [sum_over_replicas(): part = jnp.sum(exchange(blocks), axis=0)]
  transfers between devices with their start and end apart: 9 -> 10, of which waited for: 6 -> 6; matrix products, arithmetic and copies ran while one was open for 0% -> 0% of each run, Pallas kernels for 2% -> 3%
where the time goes in v2:
time: 107 us
  blocking collectives  35.5 us (33%)
  waiting for transfers between devices  26 us (24%)
  starting transfers between devices  23.7 us (22%)
  Pallas kernels  18.4 us (17%)
  local copies, waits for them, and re-layouts  1.69 us (2%)
    all_to_all x2, blocking collectives, exchange(): lax.all_to_all(blocks, 'dp', 0, 0, axis_index_groups=PLANES, tiled=True)  35.5 us
    all_to_all x2, waiting for transfers between devices, exchange(): lax.all_to_all(blocks, 'dp', 0, 0, axis_index_groups=PLANES, tiled=True)  20.4 us
    all_to_all x2, starting transfers between devices, exchange(): lax.all_to_all(blocks, 'dp', 0, 0, axis_index_groups=PLANES, tiled=True)  8.47 us
    ppermute x6, starting transfers between devices, sum_over_replicas(): met[step] = lax.ppermute(part, 'dp', partners)  6.83 us
    pallas_call x1, Pallas kernels, finish(): pl.pallas_call(kernel, grid=(MATS, ROWS // CHUNK), in_specs=[pl.BlockSpec...  6.79 us
    ppermute x1, starting transfers between devices, body(): received = lax.ppermute(other, 'tensor', PAIR)  4.67 us
    pallas_call x1, Pallas kernels, local_left(): pl.pallas_call(left_kernel, grid=(MATS,), in_specs=[pl.BlockSpec((None, N...  4.65 us
    pallas_call x1, Pallas kernels, local_right(): pl.pallas_call(right_kernel, in_specs=[pl.BlockSpec(memory_space=pltpu.SM...  4.1 us
  transfers between devices with their start and end apart: 10, of which 6 were waited for; matrix products, arithmetic and copies ran while one was open for 0% of the time, Pallas kernels for 3%

profile of v2, /device:TPU:1, one launch (start us, length us, event | category | flops | bytes accessed | tf_op | source)
XLA Modules:
  0.0 106.9 jit_solution(12781755365017375944)
XLA Ops:
  0.6 0.0 copy-start
  0.6 1.0 copy-done
  1.6 4.7 %local_left.1 = (f32[32,3,384]{2,1,0:T(4,128)S(1)}, f32[2,768,384]{2,1,0:T(8,128)S(1)}, f32[768,384]{1,0:T(8,128)}) custom-call(bf16[1,3,768,384]{3,2,1,0:T(8,128)(2,1)} %g_ref.1, f32[1,3,768,384]{3,2,1,0:T(8,128)} %e_ref.1, f32[3,32,768]{2,1,0:T(8,128)S(1)} %bitcast.3), custom_call_target="tpu_custom_call" | custom-call | tf_op jit(solution)/shard_map/left/local_left/pallas_call | solution.py:62
  6.3 21.6 %all_to_all.20 = f32[32,3,384]{2,1,0:T(4,128)S(1)} all-to-all(f32[32,3,384]{2,1,0:T(4,128)S(1)} %get-tuple-element.20), channel_id=1, replica_groups={{0,2,4,6,8,10,12,14,16,18,20,22,24,26,28,30,32,34,36,38,40,42,44,46,48,..., dimensions={0} | all-to-all | bytes 294912 | tf_op jit(solution)/shard_map/sum_left/all_to_all | solution.py:288
  27.8 0.1 reduce_sum.18
  27.9 2.8 %collective-permute-start.2 = (f32[3,384]{1,0:T(4,128)S(1)}, f32[3,384]{1,0:T(4,128)S(1)}, u32[]{:S(2)}, u32[]{:S(2)}) collective-permute-start(f32[3,384]{1,0:T(4,128)S(1)} %reduce_sum.18), channel_id=1, source_target_pairs={{0,192},{2,194},{4,196},{6,198},{8,200},{10,202},{12,204},{14,206}... | collective-permute-start | bytes 13832 | tf_op jit(solution)/shard_map/sum_left/ppermute | solution.py:306
  30.7 0.3 collective-permute-start.1
  31.1 0.3 collective-permute-start
  31.4 0.3 collective-permute-done.2
  31.7 3.0 %collective-permute-done.1 = f32[3,384]{1,0:T(4,128)S(1)} collective-permute-done((f32[3,384]{1,0:T(4,128)S(1)}, f32[3,384]{1,0:T(4,128)S(1)}, u32[]{:S(2)}, u32[]{:S(2)}) %collective-permute-start.1) | collective-permute-done | bytes 4640 | tf_op jit(solution)/shard_map/sum_left/ppermute | solution.py:306
  34.7 0.0 collective-permute-done
  34.7 0.7 broadcast_in_dim.7
  35.4 4.6 %all-to-all-start.1 = ((f32[32,3,384]{2,1,0:T(4,128)}), f32[32,3,384]{2,1,0:T(4,128)S(1)}, u32[]{:S(2)}, u32[]{:S(2)}) async-start(f32[32,3,384]{2,1,0:T(4,128)} %broadcast_in_dim.7), calls=%async_computation.1 | async-start | bytes 393216 | tf_op jit(solution)/shard_map/sum_left/all_to_all | solution.py:288
  40.0 10.0 %all-to-all-done.1.left_ref.refs_3_ = f32[32,3,384]{2,1,0:T(4,128)S(1)} async-done(((f32[32,3,384]{2,1,0:T(4,128)}), f32[32,3,384]{2,1,0:T(4,128)S(1)}, u32[]{:S(2)}, u32[]{:S(2)}) %all-to-all-start.1) | async-done | bytes 147488 | tf_op jit(solution)/shard_map/sum_left/all_to_all | solution.py:288
  50.0 4.1 %local_right.1 = (f32[32,3,384]{2,1,0:T(4,128)S(1)}, f32[32,3,512]{2,1,0:T(4,128)S(1)}, f32[32,3,128]{2,1,0:T(4,128)S(1)}) custom-call(s32[1]{0:T(128)} %bitcast.core_ref.refs_0_, f32[2,768,384]{2,1,0:T(8,128)S(1)} %get-tuple-element.18.kept_ref.refs_1_, f32[768,384]{1,0:T(8,128)} %get-tuple-element.19.stored_ref.refs_2_, ...), custom_call_target="tpu_custom_call" | custom-call | tf_op jit(solution)/shard_map/right/local_right/pallas_call | solution.py:121
  54.1 4.7 %collective-permute-start.3 = (f32[32,3,512]{2,1,0:T(4,128)S(1)}, f32[32,3,512]{2,1,0:T(4,128)S(1)}, u32[]{:S(2)}, u32[]{:S(2)}) collective-permute-start(f32[32,3,512]{2,1,0:T(4,128)S(1)} %get-tuple-element.22), channel_id=1, source_target_pairs={{0,1},{1,0},{2,3},{3,2},{4,5},{5,4},{6,7},{7,6},{8,9},{9,8},{10,11... | collective-permute-start | bytes 589832 | tf_op jit(solution)/shard_map/right/ppermute | solution.py:327
  58.8 1.2 %collective-permute-done.3 = f32[32,3,512]{2,1,0:T(4,128)S(1)} collective-permute-done((f32[32,3,512]{2,1,0:T(4,128)S(1)}, f32[32,3,512]{2,1,0:T(4,128)S(1)}, u32[]{:S(2)}, u32[]{:S(2)}) %collective-permute-start.3) | collective-permute-done | bytes 196640 | tf_op jit(solution)/shard_map/right/ppermute | solution.py:327
  59.9 0.7 slice_add_fusion
  60.7 3.9 %all-to-all-start.2 = ((f32[32,3,384]{2,1,0:T(4,128)}), f32[32,3,384]{2,1,0:T(4,128)S(1)}, u32[]{:S(2)}, u32[]{:S(2)}) async-start(f32[32,3,384]{2,1,0:T(4,128)} %slice_add_fusion), calls=%async_computation.2 | async-start | bytes 393216 | tf_op jit(solution)/shard_map/sum_right/all_to_all | solution.py:288
  64.6 10.5 %all-to-all-done.2 = f32[32,3,384]{2,1,0:T(4,128)S(1)} async-done(((f32[32,3,384]{2,1,0:T(4,128)}), f32[32,3,384]{2,1,0:T(4,128)S(1)}, u32[]{:S(2)}, u32[]{:S(2)}) %all-to-all-start.2) | async-done | bytes 147488 | tf_op jit(solution)/shard_map/sum_right/all_to_all | solution.py:288
  75.1 0.1 reduce_sum.19
  75.1 1.2 %collective-permute-start.6 = (f32[3,384]{1,0:T(4,128)S(1)}, f32[3,384]{1,0:T(4,128)S(1)}, u32[]{:S(2)}, u32[]{:S(2)}) collective-permute-start(f32[3,384]{1,0:T(4,128)S(1)} %reduce_sum.19), channel_id=1, source_target_pairs={{0,192},{2,194},{4,196},{6,198},{8,200},{10,202},{12,204},{14,206}... | collective-permute-start | bytes 13832 | tf_op jit(solution)/shard_map/sum_right/ppermute | solution.py:306
  76.3 0.7 collective-permute-start.5
  77.0 1.4 %collective-permute-start.4 = (f32[3,384]{1,0:T(4,128)S(1)}, f32[3,384]{1,0:T(4,128)S(1)}, u32[]{:S(2)}, u32[]{:S(2)}) collective-permute-start(f32[3,384]{1,0:T(4,128)S(1)} %reduce_sum.19), channel_id=1, source_target_pairs={{0,64},{2,66},{4,68},{6,70},{8,72},{10,74},{12,76},{14,78},{16,80}... | collective-permute-start | bytes 13832 | tf_op jit(solution)/shard_map/sum_right/ppermute | solution.py:306
  78.5 2.9 %inverse_factor.1.refs_6_ = f32[3,32,32]{2,1,0:T(8,128)S(1)} custom-call(f32[32,3,128]{2,1,0:T(4,128)S(1)} %slice_add_fusion.1.gram_ref), custom_call_target="tpu_custom_call" | custom-call | flops 4000000 | bytes 100000 | tf_op jit(solution)/shard_map/sum_right/inverse_factor/pallas_call | solution.py:164
  81.3 0.0 collective-permute-done.6
  81.3 0.0 collective-permute-done.5
  81.3 0.0 collective-permute-done.4
  81.4 13.9 %all_to_all.21.refs_4_ = f32[32,3,384]{2,1,0:T(4,128)S(1)} all-to-all(f32[32,3,384]{2,1,0:T(4,128)S(1)} %broadcast_in_dim.8), channel_id=1, replica_groups={{0,2,4,6,8,10,12,14,16,18,20,22,24,26,28,30,32,34,36,38,40,42,44,46,48,..., dimensions={0} | all-to-all | bytes 294912 | tf_op jit(solution)/shard_map/sum_right/all_to_all | solution.py:288
  95.3 3.7 %collective-permute-start.7 = (f32[32,3,384]{2,1,0:T(4,128)S(1)}, f32[32,3,384]{2,1,0:T(4,128)S(1)}, u32[]{:S(2)}, u32[]{:S(2)}) collective-permute-start(f32[32,3,384]{2,1,0:T(4,128)S(1)} %all_to_all.21.refs_4_), channel_id=1, source_target_pairs={{0,1},{1,0},{2,3},{3,2},{4,5},{5,4},{6,7},{7,6},{8,9},{9,8},{10,11... | collective-permute-start | bytes 442376 | tf_op jit(solution)/shard_map/sum_right/ppermute | solution.py:333
  99.1 1.1 %collective-permute-done.7.refs_5_ = f32[32,3,384]{2,1,0:T(4,128)S(1)} collective-permute-done((f32[32,3,384]{2,1,0:T(4,128)S(1)}, f32[32,3,384]{2,1,0:T(4,128)S(1)}, u32[]{:S(2)}, u32[]{:S(2)}) %collective-permute-start.7) | collective-permute-done | bytes 147488 | tf_op jit(solution)/shard_map/sum_right/ppermute | solution.py:333
  100.1 6.8 %finish.1 = (f32[1,3,768,384]{3,2,1,0:T(8,128)}, bf16[3,768,384]{2,1,0:T(8,128)(2,1)}, f32[3,32,768]{2,1,0:T(8,128)}) custom-call(s32[1]{0:T(128)} %bitcast.core_ref.refs_0_, f32[2,768,384]{2,1,0:T(8,128)S(1)} %get-tuple-element.18.kept_ref.refs_1_, f32[768,384]{1,0:T(8,128)} %get-tuple-element.19.stored_ref.refs_2_, ...), custom_call_target="tpu_custom_call" | custom-call | tf_op jit(solution)/shard_map/finish/finish/pallas_call | solution.py:253
  (4 shorter events, 0.1 us)
Async XLA Ops:
  0.6 1.0 copy-start
  27.9 3.8 %collective-permute-start.2 = (f32[3,384]{1,0:T(4,128)S(1)}, f32[3,384]{1,0:T(4,128)S(1)}, u32[]{:S(2)}, u32[]{:S(2)}) collective-permute-start(f32[3,384]{1,0:T(4,128)S(1)} %reduce_sum.18), channel_id=1, source_target_pairs={{0,192},{2,194},{4,196},{6,198},{8,200},{10,202},{12,204},{14,206}... | collective-permute-start | bytes 13832 | tf_op jit(solution)/shard_map/sum_left/ppermute | solution.py:306
  30.7 4.0 %collective-permute-start.1 = (f32[3,384]{1,0:T(4,128)S(1)}, f32[3,384]{1,0:T(4,128)S(1)}, u32[]{:S(2)}, u32[]{:S(2)}) collective-permute-start(f32[3,384]{1,0:T(4,128)S(1)} %reduce_sum.18), channel_id=1, source_target_pairs={{0,128},{2,130},{4,132},{6,134},{8,136},{10,138},{12,140},{14,142}... | collective-permute-start | bytes 13832 | tf_op jit(solution)/shard_map/sum_left/ppermute | solution.py:306
  31.1 3.6 %collective-permute-start = (f32[3,384]{1,0:T(4,128)S(1)}, f32[3,384]{1,0:T(4,128)S(1)}, u32[]{:S(2)}, u32[]{:S(2)}) collective-permute-start(f32[3,384]{1,0:T(4,128)S(1)} %reduce_sum.18), channel_id=1, source_target_pairs={{0,64},{2,66},{4,68},{6,70},{8,72},{10,74},{12,76},{14,78},{16,80}... | collective-permute-start | bytes 13832 | tf_op jit(solution)/shard_map/sum_left/ppermute | solution.py:306
  35.4 14.6 %all-to-all-start.1 = ((f32[32,3,384]{2,1,0:T(4,128)}), f32[32,3,384]{2,1,0:T(4,128)S(1)}, u32[]{:S(2)}, u32[]{:S(2)}) async-start(f32[32,3,384]{2,1,0:T(4,128)} %broadcast_in_dim.7), calls=%async_computation.1 | async-start | bytes 393216 | tf_op jit(solution)/shard_map/sum_left/all_to_all | solution.py:288
  54.1 5.8 %collective-permute-start.3 = (f32[32,3,512]{2,1,0:T(4,128)S(1)}, f32[32,3,512]{2,1,0:T(4,128)S(1)}, u32[]{:S(2)}, u32[]{:S(2)}) collective-permute-start(f32[32,3,512]{2,1,0:T(4,128)S(1)} %get-tuple-element.22), channel_id=1, source_target_pairs={{0,1},{1,0},{2,3},{3,2},{4,5},{5,4},{6,7},{7,6},{8,9},{9,8},{10,11... | collective-permute-start | bytes 589832 | tf_op jit(solution)/shard_map/right/ppermute | solution.py:327
  60.7 14.4 %all-to-all-start.2 = ((f32[32,3,384]{2,1,0:T(4,128)}), f32[32,3,384]{2,1,0:T(4,128)S(1)}, u32[]{:S(2)}, u32[]{:S(2)}) async-start(f32[32,3,384]{2,1,0:T(4,128)} %slice_add_fusion), calls=%async_computation.2 | async-start | bytes 393216 | tf_op jit(solution)/shard_map/sum_right/all_to_all | solution.py:288
  75.1 6.2 %collective-permute-start.6 = (f32[3,384]{1,0:T(4,128)S(1)}, f32[3,384]{1,0:T(4,128)S(1)}, u32[]{:S(2)}, u32[]{:S(2)}) collective-permute-start(f32[3,384]{1,0:T(4,128)S(1)} %reduce_sum.19), channel_id=1, source_target_pairs={{0,192},{2,194},{4,196},{6,198},{8,200},{10,202},{12,204},{14,206}... | collective-permute-start | bytes 13832 | tf_op jit(solution)/shard_map/sum_right/ppermute | solution.py:306
  76.3 5.0 %collective-permute-start.5 = (f32[3,384]{1,0:T(4,128)S(1)}, f32[3,384]{1,0:T(4,128)S(1)}, u32[]{:S(2)}, u32[]{:S(2)}) collective-permute-start(f32[3,384]{1,0:T(4,128)S(1)} %reduce_sum.19), channel_id=1, source_target_pairs={{0,128},{2,130},{4,132},{6,134},{8,136},{10,138},{12,140},{14,142}... | collective-permute-start | bytes 13832 | tf_op jit(solution)/shard_map/sum_right/ppermute | solution.py:306
  77.0 4.3 %collective-permute-start.4 = (f32[3,384]{1,0:T(4,128)S(1)}, f32[3,384]{1,0:T(4,128)S(1)}, u32[]{:S(2)}, u32[]{:S(2)}) collective-permute-start(f32[3,384]{1,0:T(4,128)S(1)} %reduce_sum.19), channel_id=1, source_target_pairs={{0,64},{2,66},{4,68},{6,70},{8,72},{10,74},{12,76},{14,78},{16,80}... | collective-permute-start | bytes 13832 | tf_op jit(solution)/shard_map/sum_right/ppermute | solution.py:306
  95.3 4.8 %collective-permute-start.7 = (f32[32,3,384]{2,1,0:T(4,128)S(1)}, f32[32,3,384]{2,1,0:T(4,128)S(1)}, u32[]{:S(2)}, u32[]{:S(2)}) collective-permute-start(f32[32,3,384]{2,1,0:T(4,128)S(1)} %all_to_all.21.refs_4_), channel_id=1, source_target_pairs={{0,1},{1,0},{2,3},{3,2},{4,5},{5,4},{6,7},{7,6},{8,9},{9,8},{10,11... | collective-permute-start | bytes 442376 | tf_op jit(solution)/shard_map/sum_right/ppermute | solution.py:333

commit v3 on v2

v3 whole, which is shorter than its diff:
```python
import jax
import jax.numpy as jnp
from jax import lax
from jax.experimental import pallas as pl
from jax.experimental.pallas import tpu as pltpu
from jax.sharding import PartitionSpec as P

Y, PLANE = 4, 32
PLANES = [[y * PLANE + i for i in range(PLANE)] for y in range(Y)]
PAIR = [(0, 1), (1, 0)]
MATS, ROWS, HALF, RANK = 3, 768, 384, 32
EXACT = lax.Precision.HIGHEST
KEPT = 2
ORDER = tuple(range(MATS))
CHUNK = 384
PARAMS = pltpu.CompilerParams(vmem_limit_bytes=24 * 1024 * 1024)
PARTS_LEFT = 2
PARTS_RIGHT = 2
ANYWHERE = pl.BlockSpec(memory_space=pl.ANY)
WHOLE = pl.BlockSpec(memory_space=pltpu.VMEM)


def in_hbm(x):
    return pltpu.with_memory_space_constraint(x, pltpu.HBM)


def split(x):
    high = x.astype(jnp.bfloat16)
    rest = x - high.astype(jnp.float32)
    mid = rest.astype(jnp.bfloat16)
    low = (rest - mid.astype(jnp.float32)).astype(jnp.bfloat16)
    return high, mid, low


def streamed_dot(left, merged):
    stack = jnp.concatenate(split(left), axis=0)
    flat = merged.T
    result = None
    for part in split(flat)[:PARTS_RIGHT]:
        term = jnp.dot(stack, part, preferred_element_type=jnp.float32)
        result = term if result is None else result + term
    return result[:RANK] + (result[RANK : 2 * RANK] + result[2 * RANK : 3 * RANK])


def fetches(g_ref, e_ref, g_buf, e_refs, sems, m):
    return (
        pltpu.make_async_copy(g_ref.at[0, m], g_buf, sems.at[m, 0]),
        pltpu.make_async_copy(e_ref.at[0, m], e_refs, sems.at[m, 1]),
    )


def left_kernel(g_ref, e_ref, w_ref, left_ref, kept_ref, g_buf, e_buf, w_buf, sems, w_sem):
    w_copy = pltpu.make_async_copy(w_ref, w_buf, w_sem)
    w_copy.start()
    held = [kept_ref.at[m] if m < KEPT else e_buf.at[m - KEPT] for m in range(MATS)]
    copies = [
        fetches(g_ref, e_ref, g_buf.at[m], held[m], sems, m) for m in range(MATS)
    ]
    for pair in copies:
        for copy in pair:
            copy.start()
    w_copy.wait()
    for m in range(MATS):
        stack = jnp.concatenate(split(w_buf[m]), axis=0)
        for copy in copies[m]:
            copy.wait()
        merged = g_buf[m].astype(jnp.float32) + held[m][...]
        if m < KEPT:
            kept_ref[m] = merged
        total = None
        for part in split(merged)[:PARTS_LEFT]:
            term = jnp.dot(stack, part, preferred_element_type=jnp.float32)
            total = term if total is None else total + term
        left_ref[:, m, :] = total[:RANK] + (total[RANK : 2 * RANK] + total[2 * RANK :])


def local_left(gradients, error_feedback, warm_rows):
    return pl.pallas_call(
        left_kernel,
        in_specs=[ANYWHERE] * 3,
        out_specs=[WHOLE, WHOLE],
        out_shape=[
            jax.ShapeDtypeStruct((RANK, MATS, HALF), jnp.float32),
            pltpu.VMEM((KEPT, ROWS, HALF), jnp.float32),
        ],
        scratch_shapes=[
            pltpu.VMEM((MATS, ROWS, HALF), jnp.bfloat16),
            pltpu.VMEM((MATS - KEPT, ROWS, HALF), jnp.float32),
            pltpu.VMEM((MATS, RANK, ROWS), jnp.float32),
            pltpu.SemaphoreType.DMA((MATS, 2)),
            pltpu.SemaphoreType.DMA,
        ],
        compiler_params=PARAMS,
        name="local_left",
    )(in_hbm(gradients), in_hbm(error_feedback), in_hbm(warm_rows))


def right_kernel(
    core_ref, kept_ref, g_ref, e_ref, left_ref, own_ref, other_ref, gram_ref, g_buf, e_buf, sems
):
    first = core_ref[0] == 0
    copies = {
        m: fetches(g_ref, e_ref, g_buf.at[m - KEPT], e_buf.at[m - KEPT], sems, m)
        for m in range(KEPT, MATS)
    }
    for pair in copies.values():
        for copy in pair:
            copy.start()
    for m in range(MATS):
        left = left_ref[:, m, :]
        gram = lax.dot_general(
            left,
            left,
            (((1,), (1,)), ((), ())),
            precision=EXACT,
            preferred_element_type=jnp.float32,
        )
        gram = jnp.concatenate(
            [gram, jnp.zeros((RANK, 128 - RANK), jnp.float32)], axis=1
        )
        gram_ref[:, m, :] = gram
        other_ref[:, m, HALF:] = gram
        if m < KEPT:
            merged = kept_ref[m]
        else:
            for copy in copies[m]:
                copy.wait()
            merged = g_buf[m - KEPT].astype(jnp.float32) + e_buf[m - KEPT]
        right = streamed_dot(left, merged)
        low, high = right[:, :HALF], right[:, HALF:]
        own_ref[:, m, :] = jnp.where(first, low, high)
        other_ref[:, m, :HALF] = jnp.where(first, high, low)


def local_right(core, kept, gradients, error_feedback, left):
    return pl.pallas_call(
        right_kernel,
        in_specs=[
            pl.BlockSpec(memory_space=pltpu.SMEM),
            WHOLE,
            ANYWHERE,
            ANYWHERE,
            WHOLE,
        ],
        out_specs=[WHOLE] * 3,
        out_shape=[
            jax.ShapeDtypeStruct((RANK, MATS, HALF), jnp.float32),
            jax.ShapeDtypeStruct((RANK, MATS, HALF + 128), jnp.float32),
            jax.ShapeDtypeStruct((RANK, MATS, 128), jnp.float32),
        ],
        scratch_shapes=[
            pltpu.VMEM((MATS - KEPT, ROWS, HALF), jnp.bfloat16),
            pltpu.VMEM((MATS - KEPT, ROWS, HALF), jnp.float32),
            pltpu.SemaphoreType.DMA((MATS, 2)),
        ],
        compiler_params=PARAMS,
        name="local_right",
    )(core, kept, in_hbm(gradients), in_hbm(error_feedback), left)


def inverse_kernel(gram_ref, inverse_ref):
    row = lax.broadcasted_iota(jnp.int32, (RANK, 2 * RANK), 0)
    lane = lax.broadcasted_iota(jnp.int32, (RANK, 2 * RANK), 1)
    one = (lane == row + RANK).astype(jnp.float32)[:, RANK:]
    tables, pivots = [], []
    for m in range(MATS):
        tables.append(jnp.concatenate([gram_ref[:, m, :RANK], one], axis=1))
        pivots.append(jnp.zeros((RANK, 1), jnp.float32))
    for j in range(RANK):
        for m in range(MATS):
            table = tables[m]
            pivot = table[j : j + 1, j : j + 1]
            factor = jnp.where(row[:, :1] > j, table[:, j : j + 1], 0.0) / pivot
            pivots[m] = jnp.where(row[:, :1] == j, pivot, pivots[m])
            tables[m] = table - factor * table[j : j + 1, :]
    for m in range(MATS):
        inverse_ref[m] = tables[m][:, RANK:] * lax.rsqrt(pivots[m])


def inverse_factor(gram):
    return pl.pallas_call(
        inverse_kernel,
        in_specs=[WHOLE],
        out_specs=WHOLE,
        out_shape=jax.ShapeDtypeStruct((MATS, RANK, RANK), jnp.float32),
        compiler_params=PARAMS,
        cost_estimate=pl.CostEstimate(
            flops=4_000_000, bytes_accessed=100_000, transcendentals=0
        ),
        name="inverse_factor",
    )(gram)


def finish_kernel(
    replicas,
    core_ref,
    kept_ref,
    g_ref,
    e_ref,
    left_ref,
    own_ref,
    other_ref,
    inverse_ref,
    weights_ref,
    error_ref,
    new_ref,
    right_ref,
    g_buf,
    m_buf,
    w_buf,
    e_buf,
    r_buf,
    in_sems,
    w_sems,
    out_sems,
):
    first = core_ref[0] == 0
    loads = []
    for m in range(MATS):
        pair = ()
        if m >= KEPT:
            pair = fetches(
                g_ref, e_ref, g_buf.at[m - KEPT], m_buf.at[m - KEPT], in_sems, m
            )
        loads.append(
            (pltpu.make_async_copy(weights_ref.at[m], w_buf.at[m], w_sems.at[m]), *pair)
        )
    for group in loads:
        for copy in group:
            copy.start()
    stores = []

    def store(source, target):
        copy = pltpu.make_async_copy(source, target, out_sems.at[len(stores)])
        copy.start()
        stores.append(copy)

    for m in ORDER:
        own, other = own_ref[:, m, :], other_ref[:, m, :]
        total = jnp.concatenate(
            [jnp.where(first, own, other), jnp.where(first, other, own)], axis=1
        )
        inverse = inverse_ref[m]
        right = jnp.dot(
            inverse, total, precision=EXACT, preferred_element_type=jnp.float32
        ) * (1.0 / replicas)
        basis = jnp.dot(
            inverse,
            left_ref[:, m, :],
            precision=EXACT,
            preferred_element_type=jnp.float32,
        )
        r_buf[m] = right
        store(r_buf.at[m], right_ref.at[m])
        high, mid, _ = split(right)
        rights = jnp.concatenate([high, high, mid], axis=0)
        high, mid, _ = split(basis)
        bases = jnp.concatenate([high, mid, high], axis=0)
        for copy in loads[m]:
            copy.wait()
        for c in range(ROWS // CHUNK):
            rows = pl.ds(c * CHUNK, CHUNK)
            update = lax.dot_general(
                rights[:, c * CHUNK : (c + 1) * CHUNK],
                bases,
                (((0,), (0,)), ((), ())),
                preferred_element_type=jnp.float32,
            )
            if m < KEPT:
                merged = kept_ref[m, rows, :]
            else:
                merged = g_buf[m - KEPT, rows, :].astype(jnp.float32)
                merged = merged + m_buf[m - KEPT, rows, :]
            e_buf[m, rows, :] = merged - update
            store(e_buf.at[m, rows], error_ref.at[0, m, rows])
            weights = w_buf[m, rows, :].astype(jnp.float32)
            w_buf[m, rows, :] = (weights - 0.5 * update).astype(jnp.bfloat16)
            store(w_buf.at[m, rows], new_ref.at[m, rows])
    for copy in stores:
        copy.wait()


def finish(
    core, kept, gradients, error_feedback, left, own, other, inverse, weights, replicas
):
    def kernel(*refs):
        finish_kernel(replicas, *refs)

    return pl.pallas_call(
        kernel,
        in_specs=[
            pl.BlockSpec(memory_space=pltpu.SMEM),
            WHOLE,
            ANYWHERE,
            ANYWHERE,
            WHOLE,
            WHOLE,
            WHOLE,
            WHOLE,
            ANYWHERE,
        ],
        out_specs=[ANYWHERE] * 3,
        out_shape=[
            pltpu.HBM((1, MATS, ROWS, HALF), jnp.float32),
            pltpu.HBM((MATS, ROWS, HALF), jnp.bfloat16),
            pltpu.HBM((MATS, RANK, ROWS), jnp.float32),
        ],
        scratch_shapes=[
            pltpu.VMEM((MATS - KEPT, ROWS, HALF), jnp.bfloat16),
            pltpu.VMEM((MATS - KEPT, ROWS, HALF), jnp.float32),
            pltpu.VMEM((MATS, ROWS, HALF), jnp.bfloat16),
            pltpu.VMEM((MATS, ROWS, HALF), jnp.float32),
            pltpu.VMEM((MATS, RANK, ROWS), jnp.float32),
            pltpu.SemaphoreType.DMA((MATS, 2)),
            pltpu.SemaphoreType.DMA((MATS,)),
            pltpu.SemaphoreType.DMA((MATS * (1 + 2 * ROWS // CHUNK),)),
        ],
        compiler_params=PARAMS,
        name="finish",
    )(
        core,
        kept,
        in_hbm(gradients),
        in_hbm(error_feedback),
        left,
        own,
        other,
        inverse,
        in_hbm(weights),
    )


def exchange(blocks):
    return lax.all_to_all(
        blocks, "dp", 0, 0, axis_index_groups=PLANES, tiled=True
    )


def sum_over_replicas(blocks, beside=None):
    part = jnp.sum(exchange(blocks), axis=0)
    result = None
    if beside is not None:
        work, value = beside
        part, value = lax.optimization_barrier((part, value))
    met = {}
    for step in (2, 1, 3):
        partners = [
            (y * PLANE + i, (y ^ step) * PLANE + i)
            for y in range(Y)
            for i in range(PLANE)
        ]
        met[step] = lax.ppermute(part, "dp", partners)
    if beside is not None:
        result = work(value)
        met[1], met[2], met[3], result = lax.optimization_barrier(
            (met[1], met[2], met[3], result)
        )
    total = (part + met[1]) + (met[2] + met[3])
    return exchange(jnp.broadcast_to(total[None], blocks.shape)), result


def body(gradients, error_feedback, warm_start, weights):
    replicas = lax.axis_size("dp")
    core = lax.axis_index("tensor").astype(jnp.int32)[None]
    with jax.named_scope("left"):
        blocks, kept = local_left(
            gradients, error_feedback, jnp.swapaxes(warm_start, 1, 2)
        )
    with jax.named_scope("sum_left"):
        blocks, core = lax.optimization_barrier((blocks, core))
        left, _ = sum_over_replicas(blocks)
    with jax.named_scope("right"):
        own, other, gram = local_right(core, kept, gradients, error_feedback, left)
        received = lax.ppermute(other, "tensor", PAIR)
        own, gram = lax.optimization_barrier(
            (own + received[:, :, :HALF], gram + received[:, :, HALF:])
        )
    with jax.named_scope("sum_right"):
        own, inverse = sum_over_replicas(own, (inverse_factor, gram))
        other = lax.ppermute(own, "tensor", PAIR)
    with jax.named_scope("finish"):
        next_error, new_weights, right_rows = finish(
            core,
            kept,
            gradients,
            error_feedback,
            left,
            own,
            other,
            inverse,
            weights,
            replicas,
        )
    return (next_error, new_weights, jnp.swapaxes(right_rows, 1, 2))


def solution(mesh):
    return jax.shard_map(
        body,
        mesh=mesh,
        in_specs=(
            P("dp", None, None, "tensor"),
            P("dp", None, None, "tensor"),
            P(),
            P(None, None, "tensor"),
        ),
        out_specs=(P("dp", None, None, "tensor"), P(None, None, "tensor"), P()),
        check_vma=False,
    )
```

time: 107 us -> 99 us (0.925)
  blocking collectives: 35.5 us -> 63.4 us
  waiting for transfers between devices: 26 us -> 5.55 us
  starting transfers between devices: 23.7 us -> 15.1 us
  Pallas kernels: 18.4 us -> 13.7 us
  local copies, waits for them, and re-layouts: 1.69 us -> 0.06 us
    all_to_all x2 -> x4, blocking collectives: 35.5 us -> 63.4 us  [exchange(): lax.all_to_all(blocks, 'dp', 0, 0, axis_index_groups=PLANES, tiled=True)]
    all_to_all x2 -> x0, waiting for transfers between devices: 20.4 us -> none  [exchange(): lax.all_to_all(blocks, 'dp', 0, 0, axis_index_groups=PLANES, tiled=True)]
    all_to_all x2 -> x0, starting transfers between devices: 8.47 us -> none  [exchange(): lax.all_to_all(blocks, 'dp', 0, 0, axis_index_groups=PLANES, tiled=True)]
    pallas_call x2, Pallas kernels: 11.4 us -> 7.79 us  [the longest x1 4.02 us: finish(): pl.pallas_call(kernel, in_specs=[pl.BlockSpec(memory_space=pltpu.SMEM), W...]
  transfers between devices with their start and end apart: 10 -> 8, of which waited for: 6 -> 4; matrix products, arithmetic and copies ran while one was open for 0% -> 0% of each run, Pallas kernels for 3% -> 3%
where the time goes in v3:
time: 99 us; the launch traced here: 98.7 us
  blocking collectives  63.4 us (64%)
  starting transfers between devices  15.1 us (15%)
  Pallas kernels  13.7 us (14%)
  waiting for transfers between devices  5.55 us (6%)
    all_to_all x4, blocking collectives, exchange(): lax.all_to_all(blocks, 'dp', 0, 0, axis_index_groups=PLANES, tiled=True)  63.4 us
    ppermute x6, starting transfers between devices, sum_over_replicas(): met[step] = lax.ppermute(part, 'dp', partners)  6.82 us
    ppermute x1, starting transfers between devices, body(): received = lax.ppermute(other, 'tensor', PAIR)  4.45 us
    pallas_call x1, Pallas kernels, finish(): pl.pallas_call(kernel, in_specs=[pl.BlockSpec(memory_space=pltpu.SMEM), W...  4.02 us
    ppermute x1, starting transfers between devices, body(): other = lax.ppermute(own, 'tensor', PAIR)  3.8 us
    pallas_call x1, Pallas kernels, local_left(): pl.pallas_call(left_kernel, in_specs=[ANYWHERE] * 3, out_specs=[WHOLE, WH...  3.76 us
    ppermute x6, waiting for transfers between devices, sum_over_replicas(): met[step] = lax.ppermute(part, 'dp', partners)  3.32 us
    pallas_call x1, Pallas kernels, local_right(): pl.pallas_call(right_kernel, in_specs=[pl.BlockSpec(memory_space=pltpu.SM...  3.09 us
  transfers between devices with their start and end apart: 8, of which 4 were waited for; matrix products, arithmetic and copies ran while one was open for 0% of the time, Pallas kernels for 3%

profile of v3, /device:TPU:1, one launch (start us, length us, event | category | flops | bytes accessed | tf_op | source)
XLA Modules:
  0.0 98.7 jit_solution(11702379242698701604)
XLA Ops:
  0.6 3.8 %local_left.1 = (f32[32,3,384]{2,1,0:T(4,128)S(1)}, f32[2,768,384]{2,1,0:T(8,128)S(1)}) custom-call(bf16[1,3,768,384]{3,2,1,0:T(8,128)(2,1)} %refs_2_.1, f32[1,3,768,384]{3,2,1,0:T(8,128)} %refs_3_.1, f32[3,32,768]{2,1,0:T(8,128)} %bitcast.3), custom_call_target="tpu_custom_call" | custom-call | tf_op jit(solution)/shard_map/left/local_left/pallas_call | solution.py:78
  4.4 21.6 %all_to_all.20 = f32[32,3,384]{2,1,0:T(4,128)S(1)} all-to-all(f32[32,3,384]{2,1,0:T(4,128)S(1)} %get-tuple-element.24), channel_id=1, replica_groups={{0,2,4,6,8,10,12,14,16,18,20,22,24,26,28,30,32,34,36,38,40,42,44,46,48,..., dimensions={0} | all-to-all | bytes 294912 | tf_op jit(solution)/shard_map/sum_left/all_to_all | solution.py:334
  26.0 0.1 reduce_sum.18
  26.0 2.8 %collective-permute-start.2 = (f32[3,384]{1,0:T(4,128)S(1)}, f32[3,384]{1,0:T(4,128)S(1)}, u32[]{:S(2)}, u32[]{:S(2)}) collective-permute-start(f32[3,384]{1,0:T(4,128)S(1)} %reduce_sum.18), channel_id=1, source_target_pairs={{0,192},{2,194},{4,196},{6,198},{8,200},{10,202},{12,204},{14,206}... | collective-permute-start | bytes 13832 | tf_op jit(solution)/shard_map/sum_left/ppermute | solution.py:352
  28.8 0.3 collective-permute-start.1
  29.2 0.3 collective-permute-start
  29.5 0.3 collective-permute-done.2
  29.9 3.0 %collective-permute-done.1 = f32[3,384]{1,0:T(4,128)S(1)} collective-permute-done((f32[3,384]{1,0:T(4,128)S(1)}, f32[3,384]{1,0:T(4,128)S(1)}, u32[]{:S(2)}, u32[]{:S(2)}) %collective-permute-start.1) | collective-permute-done | bytes 4640 | tf_op jit(solution)/shard_map/sum_left/ppermute | solution.py:352
  32.8 0.0 collective-permute-done
  32.9 14.3 %all_to_all.21.left_ref.refs_4_ = f32[32,3,384]{2,1,0:T(4,128)S(1)} all-to-all(f32[32,3,384]{2,1,0:T(4,128)S(1)} %broadcast_in_dim.7), channel_id=1, replica_groups={{0,2,4,6,8,10,12,14,16,18,20,22,24,26,28,30,32,34,36,38,40,42,44,46,48,..., dimensions={0} | all-to-all | bytes 294912 | tf_op jit(solution)/shard_map/sum_left/all_to_all | solution.py:334
  47.2 3.1 %local_right.1 = (f32[32,3,384]{2,1,0:T(4,128)S(1)}, f32[32,3,512]{2,1,0:T(4,128)S(1)}, f32[32,3,128]{2,1,0:T(4,128)S(1)}) custom-call(s32[1]{0:T(128)} %bitcast.1.core_ref.refs_0_, f32[2,768,384]{2,1,0:T(8,128)S(1)} %get-tuple-element.23.kept_ref.refs_1_, bf16[1,3,768,384]{3,2,1,0:T(8,128)(2,1)} %refs_2_.1, f32[1,3,768,384]{3,2,1,0:T(8,128)} %refs_3_.1, ...), custom_call_target="tpu_custom_call" | custom-call | tf_op jit(solution)/shard_map/right/local_right/pallas_call | solution.py:136
  50.3 4.4 %collective-permute-start.3 = (f32[32,3,512]{2,1,0:T(4,128)S(1)}, f32[32,3,512]{2,1,0:T(4,128)S(1)}, u32[]{:S(2)}, u32[]{:S(2)}) collective-permute-start(f32[32,3,512]{2,1,0:T(4,128)S(1)} %get-tuple-element.26), channel_id=1, source_target_pairs={{0,1},{1,0},{2,3},{3,2},{4,5},{5,4},{6,7},{7,6},{8,9},{9,8},{10,11... | collective-permute-start | bytes 589832 | tf_op jit(solution)/shard_map/right/ppermute | solution.py:374
  54.7 1.2 %collective-permute-done.3 = f32[32,3,512]{2,1,0:T(4,128)S(1)} collective-permute-done((f32[32,3,512]{2,1,0:T(4,128)S(1)}, f32[32,3,512]{2,1,0:T(4,128)S(1)}, u32[]{:S(2)}, u32[]{:S(2)}) %collective-permute-start.3) | collective-permute-done | bytes 196640 | tf_op jit(solution)/shard_map/right/ppermute | solution.py:374
  55.9 0.1 slice_add_fusion
  56.0 13.7 %all_to_all.22 = f32[32,3,384]{2,1,0:T(4,128)S(1)} all-to-all(f32[32,3,384]{2,1,0:T(4,128)S(1)} %slice_add_fusion), channel_id=1, replica_groups={{0,2,4,6,8,10,12,14,16,18,20,22,24,26,28,30,32,34,36,38,40,42,44,46,48,..., dimensions={0} | all-to-all | bytes 294912 | tf_op jit(solution)/shard_map/sum_right/all_to_all | solution.py:334
  69.7 0.1 reduce_sum.19
  69.7 1.1 %collective-permute-start.6 = (f32[3,384]{1,0:T(4,128)S(1)}, f32[3,384]{1,0:T(4,128)S(1)}, u32[]{:S(2)}, u32[]{:S(2)}) collective-permute-start(f32[3,384]{1,0:T(4,128)S(1)} %reduce_sum.19), channel_id=1, source_target_pairs={{0,192},{2,194},{4,196},{6,198},{8,200},{10,202},{12,204},{14,206}... | collective-permute-start | bytes 13832 | tf_op jit(solution)/shard_map/sum_right/ppermute | solution.py:352
  70.8 0.9 collective-permute-start.5
  71.7 1.3 %collective-permute-start.4 = (f32[3,384]{1,0:T(4,128)S(1)}, f32[3,384]{1,0:T(4,128)S(1)}, u32[]{:S(2)}, u32[]{:S(2)}) collective-permute-start(f32[3,384]{1,0:T(4,128)S(1)} %reduce_sum.19), channel_id=1, source_target_pairs={{0,64},{2,66},{4,68},{6,70},{8,72},{10,74},{12,76},{14,78},{16,80}... | collective-permute-start | bytes 13832 | tf_op jit(solution)/shard_map/sum_right/ppermute | solution.py:352
  73.1 2.9 %inverse_factor.1.refs_7_ = f32[3,32,32]{2,1,0:T(8,128)S(1)} custom-call(f32[32,3,128]{2,1,0:T(4,128)S(1)} %slice_add_fusion.1.gram_ref), custom_call_target="tpu_custom_call" | custom-call | flops 4000000 | bytes 100000 | tf_op jit(solution)/shard_map/sum_right/inverse_factor/pallas_call | solution.py:181
  75.9 0.0 collective-permute-done.6
  75.9 0.0 collective-permute-done.5
  76.0 0.0 collective-permute-done.4
  76.0 13.8 %all_to_all.23.refs_5_ = f32[32,3,384]{2,1,0:T(4,128)S(1)} all-to-all(f32[32,3,384]{2,1,0:T(4,128)S(1)} %broadcast_in_dim.8), channel_id=1, replica_groups={{0,2,4,6,8,10,12,14,16,18,20,22,24,26,28,30,32,34,36,38,40,42,44,46,48,..., dimensions={0} | all-to-all | bytes 294912 | tf_op jit(solution)/shard_map/sum_right/all_to_all | solution.py:334
  89.8 3.8 %collective-permute-start.7 = (f32[32,3,384]{2,1,0:T(4,128)S(1)}, f32[32,3,384]{2,1,0:T(4,128)S(1)}, u32[]{:S(2)}, u32[]{:S(2)}) collective-permute-start(f32[32,3,384]{2,1,0:T(4,128)S(1)} %all_to_all.23.refs_5_), channel_id=1, source_target_pairs={{0,1},{1,0},{2,3},{3,2},{4,5},{5,4},{6,7},{7,6},{8,9},{9,8},{10,11... | collective-permute-start | bytes 442376 | tf_op jit(solution)/shard_map/sum_right/ppermute | solution.py:380
  93.6 1.1 %collective-permute-done.7.refs_6_ = f32[32,3,384]{2,1,0:T(4,128)S(1)} collective-permute-done((f32[32,3,384]{2,1,0:T(4,128)S(1)}, f32[32,3,384]{2,1,0:T(4,128)S(1)}, u32[]{:S(2)}, u32[]{:S(2)}) %collective-permute-start.7) | collective-permute-done | bytes 147488 | tf_op jit(solution)/shard_map/sum_right/ppermute | solution.py:380
  94.7 4.0 %finish.1 = (f32[1,3,768,384]{3,2,1,0:T(8,128)}, bf16[3,768,384]{2,1,0:T(8,128)(2,1)}, f32[3,32,768]{2,1,0:T(8,128)}) custom-call(s32[1]{0:T(128)} %bitcast.1.core_ref.refs_0_, f32[2,768,384]{2,1,0:T(8,128)S(1)} %get-tuple-element.23.kept_ref.refs_1_, bf16[1,3,768,384]{3,2,1,0:T(8,128)(2,1)} %refs_2_.1, f32[1,3,768,384]{3,2,1,0:T(8,128)} %refs_3_.1, ...), custom_call_target="tpu_custom_call" | custom-call | tf_op jit(solution)/shard_map/finish/finish/pallas_call | solution.py:289
  (5 shorter events, 0.1 us)
Async XLA Ops:
  26.0 3.8 %collective-permute-start.2 = (f32[3,384]{1,0:T(4,128)S(1)}, f32[3,384]{1,0:T(4,128)S(1)}, u32[]{:S(2)}, u32[]{:S(2)}) collective-permute-start(f32[3,384]{1,0:T(4,128)S(1)} %reduce_sum.18), channel_id=1, source_target_pairs={{0,192},{2,194},{4,196},{6,198},{8,200},{10,202},{12,204},{14,206}... | collective-permute-start | bytes 13832 | tf_op jit(solution)/shard_map/sum_left/ppermute | solution.py:352
  28.8 4.0 %collective-permute-start.1 = (f32[3,384]{1,0:T(4,128)S(1)}, f32[3,384]{1,0:T(4,128)S(1)}, u32[]{:S(2)}, u32[]{:S(2)}) collective-permute-start(f32[3,384]{1,0:T(4,128)S(1)} %reduce_sum.18), channel_id=1, source_target_pairs={{0,128},{2,130},{4,132},{6,134},{8,136},{10,138},{12,140},{14,142}... | collective-permute-start | bytes 13832 | tf_op jit(solution)/shard_map/sum_left/ppermute | solution.py:352
  29.2 3.6 %collective-permute-start = (f32[3,384]{1,0:T(4,128)S(1)}, f32[3,384]{1,0:T(4,128)S(1)}, u32[]{:S(2)}, u32[]{:S(2)}) collective-permute-start(f32[3,384]{1,0:T(4,128)S(1)} %reduce_sum.18), channel_id=1, source_target_pairs={{0,64},{2,66},{4,68},{6,70},{8,72},{10,74},{12,76},{14,78},{16,80}... | collective-permute-start | bytes 13832 | tf_op jit(solution)/shard_map/sum_left/ppermute | solution.py:352
  50.3 5.6 %collective-permute-start.3 = (f32[32,3,512]{2,1,0:T(4,128)S(1)}, f32[32,3,512]{2,1,0:T(4,128)S(1)}, u32[]{:S(2)}, u32[]{:S(2)}) collective-permute-start(f32[32,3,512]{2,1,0:T(4,128)S(1)} %get-tuple-element.26), channel_id=1, source_target_pairs={{0,1},{1,0},{2,3},{3,2},{4,5},{5,4},{6,7},{7,6},{8,9},{9,8},{10,11... | collective-permute-start | bytes 589832 | tf_op jit(solution)/shard_map/right/ppermute | solution.py:374
  69.7 6.2 %collective-permute-start.6 = (f32[3,384]{1,0:T(4,128)S(1)}, f32[3,384]{1,0:T(4,128)S(1)}, u32[]{:S(2)}, u32[]{:S(2)}) collective-permute-start(f32[3,384]{1,0:T(4,128)S(1)} %reduce_sum.19), channel_id=1, source_target_pairs={{0,192},{2,194},{4,196},{6,198},{8,200},{10,202},{12,204},{14,206}... | collective-permute-start | bytes 13832 | tf_op jit(solution)/shard_map/sum_right/ppermute | solution.py:352
  70.8 5.1 %collective-permute-start.5 = (f32[3,384]{1,0:T(4,128)S(1)}, f32[3,384]{1,0:T(4,128)S(1)}, u32[]{:S(2)}, u32[]{:S(2)}) collective-permute-start(f32[3,384]{1,0:T(4,128)S(1)} %reduce_sum.19), channel_id=1, source_target_pairs={{0,128},{2,130},{4,132},{6,134},{8,136},{10,138},{12,140},{14,142}... | collective-permute-start | bytes 13832 | tf_op jit(solution)/shard_map/sum_right/ppermute | solution.py:352
  71.7 4.2 %collective-permute-start.4 = (f32[3,384]{1,0:T(4,128)S(1)}, f32[3,384]{1,0:T(4,128)S(1)}, u32[]{:S(2)}, u32[]{:S(2)}) collective-permute-start(f32[3,384]{1,0:T(4,128)S(1)} %reduce_sum.19), channel_id=1, source_target_pairs={{0,64},{2,66},{4,68},{6,70},{8,72},{10,74},{12,76},{14,78},{16,80}... | collective-permute-start | bytes 13832 | tf_op jit(solution)/shard_map/sum_right/ppermute | solution.py:352
  89.8 4.9 %collective-permute-start.7 = (f32[32,3,384]{2,1,0:T(4,128)S(1)}, f32[32,3,384]{2,1,0:T(4,128)S(1)}, u32[]{:S(2)}, u32[]{:S(2)}) collective-permute-start(f32[32,3,384]{2,1,0:T(4,128)S(1)} %all_to_all.23.refs_5_), channel_id=1, source_target_pairs={{0,1},{1,0},{2,3},{3,2},{4,5},{5,4},{6,7},{7,6},{8,9},{9,8},{10,11... | collective-permute-start | bytes 442376 | tf_op jit(solution)/shard_map/sum_right/ppermute | solution.py:380

commit v4 on v3

--- a/solution.py
+++ b/solution.py
@@ -5,8 +5,13 @@
 from jax.experimental.pallas import tpu as pltpu
 from jax.sharding import PartitionSpec as P
 
-Y, PLANE = 4, 32
-PLANES = [[y * PLANE + i for i in range(PLANE)] for y in range(Y)]
+Y, Z, X = 4, 8, 4
+BLOCKS = 32
+LAYERS = [
+    [(y * Z + z) * X + x for z in pair for y in range(Y) for x in range(X)]
+    for pair in ((0, 1), (3, 2), (4, 5), (7, 6))
+]
+MEETINGS = ((7, 2, 1, 4, 3, 6, 5, 0), (3, 6, 5, 0, 7, 2, 1, 4), (4, 5, 6, 7, 0, 1, 2, 3))
 PAIR = [(0, 1), (1, 0)]
 MATS, ROWS, HALF, RANK = 3, 768, 384, 32
 EXACT = lax.Precision.HIGHEST
@@ -34,12 +39,12 @@
 
 def streamed_dot(left, merged):
     stack = jnp.concatenate(split(left), axis=0)
-    flat = merged.T
-    result = None
-    for part in split(flat)[:PARTS_RIGHT]:
-        term = jnp.dot(stack, part, preferred_element_type=jnp.float32)
-        result = term if result is None else result + term
-    return result[:RANK] + (result[RANK : 2 * RANK] + result[2 * RANK : 3 * RANK])
+    result = jnp.dot(
+        jnp.concatenate([stack] * PARTS_RIGHT, axis=1),
+        jnp.concatenate(split(merged.T)[:PARTS_RIGHT], axis=0),
+        preferred_element_type=jnp.float32,
+    )
+    return result[:RANK] + (result[RANK : 2 * RANK] + result[2 * RANK :])
 
 
 def fetches(g_ref, e_ref, g_buf, e_refs, sems, m):
@@ -67,10 +72,11 @@
         merged = g_buf[m].astype(jnp.float32) + held[m][...]
         if m < KEPT:
             kept_ref[m] = merged
-        total = None
-        for part in split(merged)[:PARTS_LEFT]:
-            term = jnp.dot(stack, part, preferred_element_type=jnp.float32)
-            total = term if total is None else total + term
+        total = jnp.dot(
+            jnp.concatenate([stack] * PARTS_LEFT, axis=1),
+            jnp.concatenate(split(merged)[:PARTS_LEFT], axis=0),
+            preferred_element_type=jnp.float32,
+        )
         left_ref[:, m, :] = total[:RANK] + (total[RANK : 2 * RANK] + total[2 * RANK :])
 
 
@@ -95,46 +101,55 @@
     )(in_hbm(gradients), in_hbm(error_feedback), in_hbm(warm_rows))
 
 
-def right_kernel(
-    core_ref, kept_ref, g_ref, e_ref, left_ref, own_ref, other_ref, gram_ref, g_buf, e_buf, sems
-):
-    first = core_ref[0] == 0
-    copies = {
-        m: fetches(g_ref, e_ref, g_buf.at[m - KEPT], e_buf.at[m - KEPT], sems, m)
-        for m in range(KEPT, MATS)
-    }
-    for pair in copies.values():
-        for copy in pair:
+def right_kernel(own, *refs):
+    core_ref, kept_ref, g_ref, e_ref, left_ref, out_ref = refs[:6]
+    g_buf, e_buf, sems = refs[-3:]
+    core = core_ref[0]
+    start = (core if own else 1 - core) * HALF
+    rows = pl.ds(pl.multiple_of(start, HALF), HALF)
+    copies = {}
+    for m in range(KEPT, MATS):
+        copies[m] = (
+            pltpu.make_async_copy(g_ref.at[0, m, rows], g_buf.at[m - KEPT], sems.at[m, 0]),
+            pltpu.make_async_copy(e_ref.at[0, m, rows], e_buf.at[m - KEPT], sems.at[m, 1]),
+        )
+        for copy in copies[m]:
             copy.start()
     for m in range(MATS):
         left = left_ref[:, m, :]
-        gram = lax.dot_general(
-            left,
-            left,
-            (((1,), (1,)), ((), ())),
-            precision=EXACT,
-            preferred_element_type=jnp.float32,
-        )
-        gram = jnp.concatenate(
-            [gram, jnp.zeros((RANK, 128 - RANK), jnp.float32)], axis=1
-        )
-        gram_ref[:, m, :] = gram
-        other_ref[:, m, HALF:] = gram
+        if not own:
+            gram = lax.dot_general(
+                left,
+                left,
+                (((1,), (1,)), ((), ())),
+                precision=EXACT,
+                preferred_element_type=jnp.float32,
+            )
+            gram = jnp.concatenate(
+                [gram, jnp.zeros((RANK, 128 - RANK), jnp.float32)], axis=1
+            )
+            refs[6][:, m, :] = gram
+            out_ref[:, m, HALF:] = gram
         if m < KEPT:
-            merged = kept_ref[m]
+            merged = kept_ref[m, rows, :]
         else:
             for copy in copies[m]:
                 copy.wait()
             merged = g_buf[m - KEPT].astype(jnp.float32) + e_buf[m - KEPT]
-        right = streamed_dot(left, merged)
-        low, high = right[:, :HALF], right[:, HALF:]
-        own_ref[:, m, :] = jnp.where(first, low, high)
-        other_ref[:, m, :HALF] = jnp.where(first, high, low)
-
-
-def local_right(core, kept, gradients, error_feedback, left):
+        out_ref[:, m, :HALF] = streamed_dot(left, merged)
+
+
+def local_right(own, core, kept, gradients, error_feedback, left):
+    def kernel(*refs):
+        right_kernel(own, *refs)
+
+    half = jax.ShapeDtypeStruct((RANK, MATS, HALF), jnp.float32)
+    pair = [
+        jax.ShapeDtypeStruct((RANK, MATS, HALF + 128), jnp.float32),
+        jax.ShapeDtypeStruct((RANK, MATS, 128), jnp.float32),
+    ]
     return pl.pallas_call(
-        right_kernel,
+        kernel,
         in_specs=[
             pl.BlockSpec(memory_space=pltpu.SMEM),
             WHOLE,
@@ -142,39 +157,63 @@
             ANYWHERE,
             WHOLE,
         ],
-        out_specs=[WHOLE] * 3,
-        out_shape=[
-            jax.ShapeDtypeStruct((RANK, MATS, HALF), jnp.float32),
-            jax.ShapeDtypeStruct((RANK, MATS, HALF + 128), jnp.float32),
-            jax.ShapeDtypeStruct((RANK, MATS, 128), jnp.float32),
-        ],
+        out_specs=WHOLE if own else [WHOLE] * 2,
+        out_shape=half if own else pair,
         scratch_shapes=[
-            pltpu.VMEM((MATS - KEPT, ROWS, HALF), jnp.bfloat16),
-            pltpu.VMEM((MATS - KEPT, ROWS, HALF), jnp.float32),
+            pltpu.VMEM((MATS - KEPT, HALF, HALF), jnp.bfloat16),
+            pltpu.VMEM((MATS - KEPT, HALF, HALF), jnp.float32),
             pltpu.SemaphoreType.DMA((MATS, 2)),
         ],
         compiler_params=PARAMS,
-        name="local_right",
+        cost_estimate=pl.CostEstimate(
+            flops=200_000_000, bytes_accessed=2_000_000, transcendentals=0
+        ),
+        name="right_own" if own else "right_other",
     )(core, kept, in_hbm(gradients), in_hbm(error_feedback), left)
 
 
 def inverse_kernel(gram_ref, inverse_ref):
-    row = lax.broadcasted_iota(jnp.int32, (RANK, 2 * RANK), 0)
-    lane = lax.broadcasted_iota(jnp.int32, (RANK, 2 * RANK), 1)
-    one = (lane == row + RANK).astype(jnp.float32)[:, RANK:]
+    group, blocks = 4, RANK // 8
+    wide = (8, 2 * RANK)
+    row = lax.broadcasted_iota(jnp.int32, (RANK, RANK), 0)
+    lane = lax.broadcasted_iota(jnp.int32, (RANK, RANK), 1)
+    one = (lane == row).astype(jnp.float32)
+    below = lax.broadcasted_iota(jnp.int32, wide, 0)
     tables, pivots = [], []
     for m in range(MATS):
-        tables.append(jnp.concatenate([gram_ref[:, m, :RANK], one], axis=1))
-        pivots.append(jnp.zeros((RANK, 1), jnp.float32))
-    for j in range(RANK):
+        table = jnp.concatenate([gram_ref[:, m, :RANK], one], axis=1)
+        tables.append([table[8 * b : 8 * b + 8] for b in range(blocks)])
+        pivots.append([jnp.zeros(wide, jnp.float32)] * blocks)
+    for j in range(0, RANK, group):
+        home, at = j // 8, j % 8
+        live = range(home, blocks)
         for m in range(MATS):
             table = tables[m]
-            pivot = table[j : j + 1, j : j + 1]
-            factor = jnp.where(row[:, :1] > j, table[:, j : j + 1], 0.0) / pivot
-            pivots[m] = jnp.where(row[:, :1] == j, pivot, pivots[m])
-            tables[m] = table - factor * table[j : j + 1, :]
+            columns = [
+                {b: jnp.broadcast_to(table[b][:, j + q : j + q + 1], wide) for b in live}
+                for q in range(group)
+            ]
+            rows = [table[home][at + q : at + q + 1] for q in range(group)]
+            for q in range(group):
+                pivot = columns[q][home][at + q : at + q + 1]
+                pivots[m][home] = jnp.where(below == at + q, pivot, pivots[m][home])
+                over = 1.0 / pivot
+                scaled = rows[q] * over
+                factor = dict(columns[q])
+                factor[home] = jnp.where(below > at + q, factor[home], 0.0)
+                for later in range(q + 1, group):
+                    ratio = columns[later][home][at + q : at + q + 1] * over
+                    for b in live:
+                        columns[later][b] = columns[later][b] - factor[b] * ratio
+                    rows[later] = (
+                        rows[later] - factor[home][at + later : at + later + 1] * scaled
+                    )
+                for b in live:
+                    table[b] = table[b] - factor[b] * scaled
     for m in range(MATS):
-        inverse_ref[m] = tables[m][:, RANK:] * lax.rsqrt(pivots[m])
+        table = jnp.concatenate([block[:, RANK:] for block in tables[m]], axis=0)
+        pivot = jnp.concatenate([block[:, RANK:] for block in pivots[m]], axis=0)
+        inverse_ref[m] = table * lax.rsqrt(pivot)
 
 
 def inverse_factor(gram):
@@ -331,9 +370,7 @@
 
 
 def exchange(blocks):
-    return lax.all_to_all(
-        blocks, "dp", 0, 0, axis_index_groups=PLANES, tiled=True
-    )
+    return lax.all_to_all(blocks, "dp", 0, 0, axis_index_groups=LAYERS, tiled=True)
 
 
 def sum_over_replicas(blocks, beside=None):
@@ -342,20 +379,19 @@
     if beside is not None:
         work, value = beside
         part, value = lax.optimization_barrier((part, value))
-    met = {}
-    for step in (2, 1, 3):
+    met = []
+    for meeting in MEETINGS:
         partners = [
-            (y * PLANE + i, (y ^ step) * PLANE + i)
+            ((y * Z + z) * X + x, (y * Z + meeting[z]) * X + x)
             for y in range(Y)
-            for i in range(PLANE)
+            for z in range(Z)
+            for x in range(X)
         ]
-        met[step] = lax.ppermute(part, "dp", partners)
+        met.append(lax.ppermute(part, "dp", partners))
     if beside is not None:
         result = work(value)
-        met[1], met[2], met[3], result = lax.optimization_barrier(
-            (met[1], met[2], met[3], result)
-        )
-    total = (part + met[1]) + (met[2] + met[3])
+        *met, result = lax.optimization_barrier((*met, result))
+    total = (part + met[0]) + (met[1] + met[2])
     return exchange(jnp.broadcast_to(total[None], blocks.shape)), result
 
 
@@ -370,8 +406,9 @@
         blocks, core = lax.optimization_barrier((blocks, core))
         left, _ = sum_over_replicas(blocks)
     with jax.named_scope("right"):
-        own, other, gram = local_right(core, kept, gradients, error_feedback, left)
+        other, gram = local_right(False, core, kept, gradients, error_feedback, left)
         received = lax.ppermute(other, "tensor", PAIR)
+        own = local_right(True, core, kept, gradients, error_feedback, left)
         own, gram = lax.optimization_barrier(
             (own + received[:, :, :HALF], gram + received[:, :, HALF:])
         )

time: 99 us -> 92.2 us (0.931)
  blocking collectives: 63.4 us -> 50.4 us
  starting transfers between devices: 15.1 us -> 22.6 us
  Pallas kernels: 13.7 us -> 12.5 us
    all_to_all x4, blocking collectives: 63.4 us -> 50.4 us  [exchange(): lax.all_to_all(blocks, 'dp', 0, 0, axis_index_groups=LAYERS, tiled=True)]
    ppermute x6, starting transfers between devices: 6.82 us -> 13.5 us  [sum_over_replicas(): met.append(lax.ppermute(part, 'dp', partners))]
    pallas_call x1, Pallas kernels: 2.87 us -> 1.33 us  [inverse_factor(): pl.pallas_call(inverse_kernel, in_specs=[WHOLE], out_specs=WHOLE, out_sha...]
    ppermute x1, waiting for transfers between devices: 1.16 us -> 0.01 us  [body(): received = lax.ppermute(other, 'tensor', PAIR)]
    ppermute x6, waiting for transfers between devices: 3.32 us -> 4.37 us  [sum_over_replicas(): met.append(lax.ppermute(part, 'dp', partners))]
    pallas_call x1 -> x2, Pallas kernels: 3.09 us -> 3.61 us  [local_right(): pl.pallas_call(kernel, in_specs=[pl.BlockSpec(memory_space=pltpu.SMEM), W...]
where the time goes in v4:
time: 92.2 us; the launch traced here: 91.9 us
  blocking collectives  50.4 us (55%)
  starting transfers between devices  22.6 us (25%)
  Pallas kernels  12.5 us (14%)
  waiting for transfers between devices  5.45 us (6%)
    all_to_all x4, blocking collectives, exchange(): lax.all_to_all(blocks, 'dp', 0, 0, axis_index_groups=LAYERS, tiled=True)  50.4 us
    ppermute x6, starting transfers between devices, sum_over_replicas(): met.append(lax.ppermute(part, 'dp', partners))  13.5 us
    ppermute x1, starting transfers between devices, body(): received = lax.ppermute(other, 'tensor', PAIR)  5 us
    ppermute x6, waiting for transfers between devices, sum_over_replicas(): met.append(lax.ppermute(part, 'dp', partners))  4.37 us
    ppermute x1, starting transfers between devices, body(): other = lax.ppermute(own, 'tensor', PAIR)  4.14 us
    pallas_call x1, Pallas kernels, finish(): pl.pallas_call(kernel, in_specs=[pl.BlockSpec(memory_space=pltpu.SMEM), W...  4.02 us
    pallas_call x2, Pallas kernels, local_right(): pl.pallas_call(kernel, in_specs=[pl.BlockSpec(memory_space=pltpu.SMEM), W...  3.61 us
    pallas_call x1, Pallas kernels, local_left(): pl.pallas_call(left_kernel, in_specs=[ANYWHERE] * 3, out_specs=[WHOLE, WH...  3.55 us
  transfers between devices with their start and end apart: 8, of which 4 were waited for; matrix products, arithmetic and copies ran while one was open for 0% of the time, Pallas kernels for 3%

profile of v4, /device:TPU:1, one launch (start us, length us, event | category | flops | bytes accessed | tf_op | source)
XLA Modules:
  0.0 91.9 jit_solution(14473459530684610712)
XLA Ops:
  0.6 3.6 %local_left.1 = (f32[32,3,384]{2,1,0:T(4,128)S(1)}, f32[2,768,384]{2,1,0:T(8,128)S(1)}) custom-call(bf16[1,3,768,384]{3,2,1,0:T(8,128)(2,1)} %refs_2_.5, f32[1,3,768,384]{3,2,1,0:T(8,128)} %refs_3_.5, f32[3,32,768]{2,1,0:T(8,128)} %bitcast.3), custom_call_target="tpu_custom_call" | custom-call | tf_op jit(solution)/shard_map/left/local_left/pallas_call | solution.py:84
  4.2 16.7 %all_to_all.20 = f32[32,3,384]{2,1,0:T(4,128)S(1)} all-to-all(f32[32,3,384]{2,1,0:T(4,128)S(1)} %get-tuple-element.23), channel_id=1, replica_groups={{0,2,4,6,64,66,68,70,128,130,132,134,192,194,196,198,8,10,12,14,72,74,7..., dimensions={0} | all-to-all | bytes 294912 | tf_op jit(solution)/shard_map/sum_left/all_to_all | solution.py:373
  20.9 0.1 reduce_sum.18
  21.0 6.1 %collective-permute-start.2 = (f32[3,384]{1,0:T(4,128)S(1)}, f32[3,384]{1,0:T(4,128)S(1)}, u32[]{:S(2)}, u32[]{:S(2)}) collective-permute-start(f32[3,384]{1,0:T(4,128)S(1)} %reduce_sum.18), channel_id=1, source_target_pairs={{0,32},{2,34},{4,36},{6,38},{8,40},{10,42},{12,44},{14,46},{16,48}... | collective-permute-start | bytes 13832 | tf_op jit(solution)/shard_map/sum_left/ppermute | solution.py:390
  27.1 1.6 %collective-permute-start.1 = (f32[3,384]{1,0:T(4,128)S(1)}, f32[3,384]{1,0:T(4,128)S(1)}, u32[]{:S(2)}, u32[]{:S(2)}) collective-permute-start(f32[3,384]{1,0:T(4,128)S(1)} %reduce_sum.18), channel_id=1, source_target_pairs={{0,24},{2,26},{4,28},{6,30},{8,48},{10,50},{12,52},{14,54},{16,40}... | collective-permute-start | bytes 13832 | tf_op jit(solution)/shard_map/sum_left/ppermute | solution.py:390
  28.7 0.0 collective-permute-start
  28.7 0.0 collective-permute-done.2
  28.7 2.6 %collective-permute-done.1 = f32[3,384]{1,0:T(4,128)S(1)} collective-permute-done((f32[3,384]{1,0:T(4,128)S(1)}, f32[3,384]{1,0:T(4,128)S(1)}, u32[]{:S(2)}, u32[]{:S(2)}) %collective-permute-start.1) | collective-permute-done | bytes 4640 | tf_op jit(solution)/shard_map/sum_left/ppermute | solution.py:390
  31.3 1.0 %collective-permute-done = f32[3,384]{1,0:T(4,128)S(1)} collective-permute-done((f32[3,384]{1,0:T(4,128)S(1)}, f32[3,384]{1,0:T(4,128)S(1)}, u32[]{:S(2)}, u32[]{:S(2)}) %collective-permute-start) | collective-permute-done | bytes 4640 | tf_op jit(solution)/shard_map/sum_left/ppermute | solution.py:390
  32.4 11.3 %all_to_all.21.refs_4_ = f32[32,3,384]{2,1,0:T(4,128)S(1)} all-to-all(f32[32,3,384]{2,1,0:T(4,128)S(1)} %broadcast_in_dim.7), channel_id=1, replica_groups={{0,2,4,6,64,66,68,70,128,130,132,134,192,194,196,198,8,10,12,14,72,74,7..., dimensions={0} | all-to-all | bytes 294912 | tf_op jit(solution)/shard_map/sum_left/all_to_all | solution.py:373
  43.7 1.8 %right_other.1 = (f32[32,3,512]{2,1,0:T(4,128)S(1)}, f32[32,3,128]{2,1,0:T(4,128)S(1)}) custom-call(s32[1]{0:T(128)} %bitcast.1.refs_0_, f32[2,768,384]{2,1,0:T(8,128)S(1)} %get-tuple-element.22.refs_1_, bf16[1,3,768,384]{3,2,1,0:T(8,128)(2,1)} %refs_2_.5, f32[1,3,768,384]{3,2,1,0:T(8,128)} %refs_3_.5, f32[32,3,384]{2,1,0:T(4,128)S(1)} %all_to_all.21.refs_4_), custom_call_target="tpu_custom_call" | custom-call | flops 200000000 | bytes 2000000 | tf_op jit(solution)/shard_map/right/right_other/pallas_call | solution.py:151
  45.5 5.0 %collective-permute-start.3 = (f32[32,3,512]{2,1,0:T(4,128)S(1)}, f32[32,3,512]{2,1,0:T(4,128)S(1)}, u32[]{:S(2)}, u32[]{:S(2)}) collective-permute-start(f32[32,3,512]{2,1,0:T(4,128)S(1)} %get-tuple-element.24), channel_id=1, source_target_pairs={{0,1},{1,0},{2,3},{3,2},{4,5},{5,4},{6,7},{7,6},{8,9},{9,8},{10,11... | collective-permute-start | bytes 589832 | tf_op jit(solution)/shard_map/right/ppermute | solution.py:410
  50.5 1.8 %right_own.1 = f32[32,3,384]{2,1,0:T(4,128)S(1)} custom-call(s32[1]{0:T(128)} %bitcast.1.refs_0_, f32[2,768,384]{2,1,0:T(8,128)S(1)} %get-tuple-element.22.refs_1_, bf16[1,3,768,384]{3,2,1,0:T(8,128)(2,1)} %refs_2_.5, f32[1,3,768,384]{3,2,1,0:T(8,128)} %refs_3_.5, f32[32,3,384]{2,1,0:T(4,128)S(1)} %all_to_all.21.refs_4_), custom_call_target="tpu_custom_call" | custom-call | flops 200000000 | bytes 2000000 | tf_op jit(solution)/shard_map/right/right_own/pallas_call | solution.py:151
  52.3 0.0 collective-permute-done.3
  52.4 0.1 slice_add_fusion
  52.4 11.3 %all_to_all.22 = f32[32,3,384]{2,1,0:T(4,128)S(1)} all-to-all(f32[32,3,384]{2,1,0:T(4,128)S(1)} %slice_add_fusion), channel_id=1, replica_groups={{0,2,4,6,64,66,68,70,128,130,132,134,192,194,196,198,8,10,12,14,72,74,7..., dimensions={0} | all-to-all | bytes 294912 | tf_op jit(solution)/shard_map/sum_right/all_to_all | solution.py:373
  63.8 0.1 reduce_sum.19
  63.8 2.1 %collective-permute-start.6 = (f32[3,384]{1,0:T(4,128)S(1)}, f32[3,384]{1,0:T(4,128)S(1)}, u32[]{:S(2)}, u32[]{:S(2)}) collective-permute-start(f32[3,384]{1,0:T(4,128)S(1)} %reduce_sum.19), channel_id=1, source_target_pairs={{0,32},{2,34},{4,36},{6,38},{8,40},{10,42},{12,44},{14,46},{16,48}... | collective-permute-start | bytes 13832 | tf_op jit(solution)/shard_map/sum_right/ppermute | solution.py:390
  66.0 1.6 %collective-permute-start.5 = (f32[3,384]{1,0:T(4,128)S(1)}, f32[3,384]{1,0:T(4,128)S(1)}, u32[]{:S(2)}, u32[]{:S(2)}) collective-permute-start(f32[3,384]{1,0:T(4,128)S(1)} %reduce_sum.19), channel_id=1, source_target_pairs={{0,24},{2,26},{4,28},{6,30},{8,48},{10,50},{12,52},{14,54},{16,40}... | collective-permute-start | bytes 13832 | tf_op jit(solution)/shard_map/sum_right/ppermute | solution.py:390
  67.6 2.0 %collective-permute-start.4 = (f32[3,384]{1,0:T(4,128)S(1)}, f32[3,384]{1,0:T(4,128)S(1)}, u32[]{:S(2)}, u32[]{:S(2)}) collective-permute-start(f32[3,384]{1,0:T(4,128)S(1)} %reduce_sum.19), channel_id=1, source_target_pairs={{0,56},{2,58},{4,60},{6,62},{8,16},{10,18},{12,20},{14,22},{16,8},... | collective-permute-start | bytes 13832 | tf_op jit(solution)/shard_map/sum_right/ppermute | solution.py:390
  69.6 1.3 %inverse_factor.1.refs_7_ = f32[3,32,32]{2,1,0:T(8,128)S(1)} custom-call(f32[32,3,128]{2,1,0:T(4,128)S(1)} %slice_add_fusion.1.gram_ref), custom_call_target="tpu_custom_call" | custom-call | flops 4000000 | bytes 100000 | tf_op jit(solution)/shard_map/sum_right/inverse_factor/pallas_call | solution.py:220
  70.9 0.0 collective-permute-done.6
  70.9 0.0 collective-permute-done.5
  70.9 0.7 collective-permute-done.4
  71.6 11.1 %all_to_all.23.refs_5_ = f32[32,3,384]{2,1,0:T(4,128)S(1)} all-to-all(f32[32,3,384]{2,1,0:T(4,128)S(1)} %broadcast_in_dim.8), channel_id=1, replica_groups={{0,2,4,6,64,66,68,70,128,130,132,134,192,194,196,198,8,10,12,14,72,74,7..., dimensions={0} | all-to-all | bytes 294912 | tf_op jit(solution)/shard_map/sum_right/all_to_all | solution.py:373
  82.7 4.1 %collective-permute-start.7 = (f32[32,3,384]{2,1,0:T(4,128)S(1)}, f32[32,3,384]{2,1,0:T(4,128)S(1)}, u32[]{:S(2)}, u32[]{:S(2)}) collective-permute-start(f32[32,3,384]{2,1,0:T(4,128)S(1)} %all_to_all.23.refs_5_), channel_id=1, source_target_pairs={{0,1},{1,0},{2,3},{3,2},{4,5},{5,4},{6,7},{7,6},{8,9},{9,8},{10,11... | collective-permute-start | bytes 442376 | tf_op jit(solution)/shard_map/sum_right/ppermute | solution.py:417
  86.8 1.1 %collective-permute-done.7.refs_6_ = f32[32,3,384]{2,1,0:T(4,128)S(1)} collective-permute-done((f32[32,3,384]{2,1,0:T(4,128)S(1)}, f32[32,3,384]{2,1,0:T(4,128)S(1)}, u32[]{:S(2)}, u32[]{:S(2)}) %collective-permute-start.7) | collective-permute-done | bytes 147488 | tf_op jit(solution)/shard_map/sum_right/ppermute | solution.py:417
  87.9 4.0 %finish.1 = (f32[1,3,768,384]{3,2,1,0:T(8,128)}, bf16[3,768,384]{2,1,0:T(8,128)(2,1)}, f32[3,32,768]{2,1,0:T(8,128)}) custom-call(s32[1]{0:T(128)} %bitcast.1.refs_0_, f32[2,768,384]{2,1,0:T(8,128)S(1)} %get-tuple-element.22.refs_1_, bf16[1,3,768,384]{3,2,1,0:T(8,128)(2,1)} %refs_2_.5, f32[1,3,768,384]{3,2,1,0:T(8,128)} %refs_3_.5, ...), custom_call_target="tpu_custom_call" | custom-call | tf_op jit(solution)/shard_map/finish/finish/pallas_call | solution.py:328
  (5 shorter events, 0.1 us)
Async XLA Ops:
  21.0 7.7 %collective-permute-start.2 = (f32[3,384]{1,0:T(4,128)S(1)}, f32[3,384]{1,0:T(4,128)S(1)}, u32[]{:S(2)}, u32[]{:S(2)}) collective-permute-start(f32[3,384]{1,0:T(4,128)S(1)} %reduce_sum.18), channel_id=1, source_target_pairs={{0,32},{2,34},{4,36},{6,38},{8,40},{10,42},{12,44},{14,46},{16,48}... | collective-permute-start | bytes 13832 | tf_op jit(solution)/shard_map/sum_left/ppermute | solution.py:390
  27.1 4.3 %collective-permute-start.1 = (f32[3,384]{1,0:T(4,128)S(1)}, f32[3,384]{1,0:T(4,128)S(1)}, u32[]{:S(2)}, u32[]{:S(2)}) collective-permute-start(f32[3,384]{1,0:T(4,128)S(1)} %reduce_sum.18), channel_id=1, source_target_pairs={{0,24},{2,26},{4,28},{6,30},{8,48},{10,50},{12,52},{14,54},{16,40}... | collective-permute-start | bytes 13832 | tf_op jit(solution)/shard_map/sum_left/ppermute | solution.py:390
  28.7 3.7 %collective-permute-start = (f32[3,384]{1,0:T(4,128)S(1)}, f32[3,384]{1,0:T(4,128)S(1)}, u32[]{:S(2)}, u32[]{:S(2)}) collective-permute-start(f32[3,384]{1,0:T(4,128)S(1)} %reduce_sum.18), channel_id=1, source_target_pairs={{0,56},{2,58},{4,60},{6,62},{8,16},{10,18},{12,20},{14,22},{16,8},... | collective-permute-start | bytes 13832 | tf_op jit(solution)/shard_map/sum_left/ppermute | solution.py:390
  45.5 6.8 %collective-permute-start.3 = (f32[32,3,512]{2,1,0:T(4,128)S(1)}, f32[32,3,512]{2,1,0:T(4,128)S(1)}, u32[]{:S(2)}, u32[]{:S(2)}) collective-permute-start(f32[32,3,512]{2,1,0:T(4,128)S(1)} %get-tuple-element.24), channel_id=1, source_target_pairs={{0,1},{1,0},{2,3},{3,2},{4,5},{5,4},{6,7},{7,6},{8,9},{9,8},{10,11... | collective-permute-start | bytes 589832 | tf_op jit(solution)/shard_map/right/ppermute | solution.py:410
  63.8 7.1 %collective-permute-start.6 = (f32[3,384]{1,0:T(4,128)S(1)}, f32[3,384]{1,0:T(4,128)S(1)}, u32[]{:S(2)}, u32[]{:S(2)}) collective-permute-start(f32[3,384]{1,0:T(4,128)S(1)} %reduce_sum.19), channel_id=1, source_target_pairs={{0,32},{2,34},{4,36},{6,38},{8,40},{10,42},{12,44},{14,46},{16,48}... | collective-permute-start | bytes 13832 | tf_op jit(solution)/shard_map/sum_right/ppermute | solution.py:390
  66.0 4.9 %collective-permute-start.5 = (f32[3,384]{1,0:T(4,128)S(1)}, f32[3,384]{1,0:T(4,128)S(1)}, u32[]{:S(2)}, u32[]{:S(2)}) collective-permute-start(f32[3,384]{1,0:T(4,128)S(1)} %reduce_sum.19), channel_id=1, source_target_pairs={{0,24},{2,26},{4,28},{6,30},{8,48},{10,50},{12,52},{14,54},{16,40}... | collective-permute-start | bytes 13832 | tf_op jit(solution)/shard_map/sum_right/ppermute | solution.py:390
  67.6 4.0 %collective-permute-start.4 = (f32[3,384]{1,0:T(4,128)S(1)}, f32[3,384]{1,0:T(4,128)S(1)}, u32[]{:S(2)}, u32[]{:S(2)}) collective-permute-start(f32[3,384]{1,0:T(4,128)S(1)} %reduce_sum.19), channel_id=1, source_target_pairs={{0,56},{2,58},{4,60},{6,62},{8,16},{10,18},{12,20},{14,22},{16,8},... | collective-permute-start | bytes 13832 | tf_op jit(solution)/shard_map/sum_right/ppermute | solution.py:390
  82.7 5.2 %collective-permute-start.7 = (f32[32,3,384]{2,1,0:T(4,128)S(1)}, f32[32,3,384]{2,1,0:T(4,128)S(1)}, u32[]{:S(2)}, u32[]{:S(2)}) collective-permute-start(f32[32,3,384]{2,1,0:T(4,128)S(1)} %all_to_all.23.refs_5_), channel_id=1, source_target_pairs={{0,1},{1,0},{2,3},{3,2},{4,5},{5,4},{6,7},{7,6},{8,9},{9,8},{10,11... | collective-permute-start | bytes 442376 | tf_op jit(solution)/shard_map/sum_right/ppermute | solution.py:417

commit v5 on v4

--- a/solution.py
+++ b/solution.py
@@ -14,6 +14,7 @@
 MEETINGS = ((7, 2, 1, 4, 3, 6, 5, 0), (3, 6, 5, 0, 7, 2, 1, 4), (4, 5, 6, 7, 0, 1, 2, 3))
 PAIR = [(0, 1), (1, 0)]
 MATS, ROWS, HALF, RANK = 3, 768, 384, 32
+WIDTH = MATS * HALF
 EXACT = lax.Precision.HIGHEST
 KEPT = 2
 ORDER = tuple(range(MATS))
@@ -25,6 +26,10 @@
 WHOLE = pl.BlockSpec(memory_space=pltpu.VMEM)
 
 
+def at(m):
+    return slice(m * HALF, (m + 1) * HALF)
+
+
 def in_hbm(x):
     return pltpu.with_memory_space_constraint(x, pltpu.HBM)
 
@@ -38,6 +43,17 @@
 
 
 def streamed_dot(left, merged):
+    high, mid, low = split(left.T)
+    stack = jnp.concatenate([high, mid, low, jnp.zeros_like(low)], axis=1)
+    result = jnp.dot(
+        jnp.concatenate(split(merged)[:PARTS_RIGHT], axis=1),
+        jnp.concatenate([stack] * PARTS_RIGHT, axis=0),
+        preferred_element_type=jnp.float32,
+    ).T
+    return result[:RANK] + (result[RANK : 2 * RANK] + result[2 * RANK : 3 * RANK])
+
+
+def turned_dot(left, merged):
     stack = jnp.concatenate(split(left), axis=0)
     result = jnp.dot(
         jnp.concatenate([stack] * PARTS_RIGHT, axis=1),
@@ -54,7 +70,13 @@
     )
 
 
-def left_kernel(g_ref, e_ref, w_ref, left_ref, kept_ref, g_buf, e_buf, w_buf, sems, w_sem):
+def half_of(core, own):
+    return pl.ds(pl.multiple_of((core if own else 1 - core) * HALF, HALF), HALF)
+
+
+def left_kernel(
+    core_ref, g_ref, e_ref, w_ref, left_ref, kept_ref, half_ref, g_buf, e_buf, w_buf, sems, w_sem
+):
     w_copy = pltpu.make_async_copy(w_ref, w_buf, w_sem)
     w_copy.start()
     held = [kept_ref.at[m] if m < KEPT else e_buf.at[m - KEPT] for m in range(MATS)]
@@ -72,22 +94,26 @@
         merged = g_buf[m].astype(jnp.float32) + held[m][...]
         if m < KEPT:
             kept_ref[m] = merged
+        else:
+            first = core_ref[0] == 0
+            half_ref[m - KEPT] = jnp.where(first, merged[HALF:], merged[:HALF])
         total = jnp.dot(
             jnp.concatenate([stack] * PARTS_LEFT, axis=1),
             jnp.concatenate(split(merged)[:PARTS_LEFT], axis=0),
             preferred_element_type=jnp.float32,
         )
-        left_ref[:, m, :] = total[:RANK] + (total[RANK : 2 * RANK] + total[2 * RANK :])
-
-
-def local_left(gradients, error_feedback, warm_rows):
+        left_ref[:, 0, at(m)] = total[:RANK] + (total[RANK : 2 * RANK] + total[2 * RANK :])
+
+
+def local_left(core, gradients, error_feedback, warm_rows):
     return pl.pallas_call(
         left_kernel,
-        in_specs=[ANYWHERE] * 3,
-        out_specs=[WHOLE, WHOLE],
+        in_specs=[pl.BlockSpec(memory_space=pltpu.SMEM)] + [ANYWHERE] * 3,
+        out_specs=[WHOLE] * 3,
         out_shape=[
-            jax.ShapeDtypeStruct((RANK, MATS, HALF), jnp.float32),
+            pltpu.VMEM((RANK, 1, WIDTH), jnp.float32),
             pltpu.VMEM((KEPT, ROWS, HALF), jnp.float32),
+            pltpu.VMEM((MATS - KEPT, HALF, HALF), jnp.float32),
         ],
         scratch_shapes=[
             pltpu.VMEM((MATS, ROWS, HALF), jnp.bfloat16),
@@ -98,15 +124,33 @@
         ],
         compiler_params=PARAMS,
         name="local_left",
-    )(in_hbm(gradients), in_hbm(error_feedback), in_hbm(warm_rows))
-
-
-def right_kernel(own, *refs):
-    core_ref, kept_ref, g_ref, e_ref, left_ref, out_ref = refs[:6]
-    g_buf, e_buf, sems = refs[-3:]
-    core = core_ref[0]
-    start = (core if own else 1 - core) * HALF
-    rows = pl.ds(pl.multiple_of(start, HALF), HALF)
+    )(core, in_hbm(gradients), in_hbm(error_feedback), in_hbm(warm_rows))
+
+
+def right_other_kernel(core_ref, kept_ref, half_ref, left_ref, out_ref, gram_ref):
+    rows = half_of(core_ref[0], False)
+    for m in range(MATS):
+        left = left_ref[:, 0, at(m)]
+        gram = lax.dot_general(
+            left,
+            left,
+            (((1,), (1,)), ((), ())),
+            precision=EXACT,
+            preferred_element_type=jnp.float32,
+        )
+        gram = jnp.concatenate(
+            [gram, jnp.zeros((RANK, 128 - RANK), jnp.float32)], axis=1
+        )
+        gram_ref[:, 0, m * 128 : (m + 1) * 128] = gram
+        out_ref[:, 0, WIDTH + m * 128 : WIDTH + (m + 1) * 128] = gram
+        merged = kept_ref[m, rows, :] if m < KEPT else half_ref[m - KEPT]
+        out_ref[:, 0, at(m)] = streamed_dot(left, merged)
+
+
+def right_own_kernel(
+    core_ref, kept_ref, g_ref, e_ref, left_ref, out_ref, g_buf, e_buf, sems
+):
+    rows = half_of(core_ref[0], True)
     copies = {}
     for m in range(KEPT, MATS):
         copies[m] = (
@@ -116,40 +160,32 @@
         for copy in copies[m]:
             copy.start()
     for m in range(MATS):
-        left = left_ref[:, m, :]
-        if not own:
-            gram = lax.dot_general(
-                left,
-                left,
-                (((1,), (1,)), ((), ())),
-                precision=EXACT,
-                preferred_element_type=jnp.float32,
-            )
-            gram = jnp.concatenate(
-                [gram, jnp.zeros((RANK, 128 - RANK), jnp.float32)], axis=1
-            )
-            refs[6][:, m, :] = gram
-            out_ref[:, m, HALF:] = gram
         if m < KEPT:
             merged = kept_ref[m, rows, :]
         else:
             for copy in copies[m]:
                 copy.wait()
             merged = g_buf[m - KEPT].astype(jnp.float32) + e_buf[m - KEPT]
-        out_ref[:, m, :HALF] = streamed_dot(left, merged)
-
-
-def local_right(own, core, kept, gradients, error_feedback, left):
-    def kernel(*refs):
-        right_kernel(own, *refs)
-
-    half = jax.ShapeDtypeStruct((RANK, MATS, HALF), jnp.float32)
-    pair = [
-        jax.ShapeDtypeStruct((RANK, MATS, HALF + 128), jnp.float32),
-        jax.ShapeDtypeStruct((RANK, MATS, 128), jnp.float32),
-    ]
+        out_ref[:, 0, at(m)] = turned_dot(left_ref[:, 0, at(m)], merged)
+
+
+def right_other(core, kept, half, left):
     return pl.pallas_call(
-        kernel,
+        right_other_kernel,
+        in_specs=[pl.BlockSpec(memory_space=pltpu.SMEM)] + [WHOLE] * 3,
+        out_specs=[WHOLE] * 2,
+        out_shape=[
+            pltpu.VMEM((RANK, 1, WIDTH + MATS * 128), jnp.float32),
+            pltpu.VMEM((RANK, 1, MATS * 128), jnp.float32),
+        ],
+        compiler_params=PARAMS,
+        name="right_other",
+    )(core, kept, half, left)
+
+
+def right_own(core, kept, gradients, error_feedback, left):
+    return pl.pallas_call(
+        right_own_kernel,
         in_specs=[
             pl.BlockSpec(memory_space=pltpu.SMEM),
             WHOLE,
@@ -157,8 +193,8 @@
             ANYWHERE,
             WHOLE,
         ],
-        out_specs=WHOLE if own else [WHOLE] * 2,
-        out_shape=half if own else pair,
+        out_specs=WHOLE,
+        out_shape=pltpu.VMEM((RANK, 1, WIDTH), jnp.float32),
         scratch_shapes=[
             pltpu.VMEM((MATS - KEPT, HALF, HALF), jnp.bfloat16),
             pltpu.VMEM((MATS - KEPT, HALF, HALF), jnp.float32),
@@ -168,7 +204,7 @@
         cost_estimate=pl.CostEstimate(
             flops=200_000_000, bytes_accessed=2_000_000, transcendentals=0
         ),
-        name="right_own" if own else "right_other",
+        name="right_own",
     )(core, kept, in_hbm(gradients), in_hbm(error_feedback), left)
 
 
@@ -181,7 +217,7 @@
     below = lax.broadcasted_iota(jnp.int32, wide, 0)
     tables, pivots = [], []
     for m in range(MATS):
-        table = jnp.concatenate([gram_ref[:, m, :RANK], one], axis=1)
+        table = jnp.concatenate([gram_ref[:, 0, m * 128 : m * 128 + RANK], one], axis=1)
         tables.append([table[8 * b : 8 * b + 8] for b in range(blocks)])
         pivots.append([jnp.zeros(wide, jnp.float32)] * blocks)
     for j in range(0, RANK, group):
@@ -275,7 +311,7 @@
         stores.append(copy)
 
     for m in ORDER:
-        own, other = own_ref[:, m, :], other_ref[:, m, :]
+        own, other = own_ref[:, 0, at(m)], other_ref[:, 0, at(m)]
         total = jnp.concatenate(
             [jnp.where(first, own, other), jnp.where(first, other, own)], axis=1
         )
@@ -285,7 +321,7 @@
         ) * (1.0 / replicas)
         basis = jnp.dot(
             inverse,
-            left_ref[:, m, :],
+            left_ref[:, 0, at(m)],
             precision=EXACT,
             preferred_element_type=jnp.float32,
         )
@@ -399,18 +435,18 @@
     replicas = lax.axis_size("dp")
     core = lax.axis_index("tensor").astype(jnp.int32)[None]
     with jax.named_scope("left"):
-        blocks, kept = local_left(
-            gradients, error_feedback, jnp.swapaxes(warm_start, 1, 2)
+        blocks, kept, half = local_left(
+            core, gradients, error_feedback, jnp.swapaxes(warm_start, 1, 2)
         )
     with jax.named_scope("sum_left"):
         blocks, core = lax.optimization_barrier((blocks, core))
         left, _ = sum_over_replicas(blocks)
     with jax.named_scope("right"):
-        other, gram = local_right(False, core, kept, gradients, error_feedback, left)
+        other, gram = right_other(core, kept, half, left)
         received = lax.ppermute(other, "tensor", PAIR)
-        own = local_right(True, core, kept, gradients, error_feedback, left)
+        own = right_own(core, kept, gradients, error_feedback, left)
         own, gram = lax.optimization_barrier(
-            (own + received[:, :, :HALF], gram + received[:, :, HALF:])
+            (own + received[:, :, :WIDTH], gram + received[:, :, WIDTH:])
         )
     with jax.named_scope("sum_right"):
         own, inverse = sum_over_replicas(own, (inverse_factor, gram))

time: 92.2 us -> 91 us (0.987)
  blocking collectives: 50.4 us -> 49.4 us
    all_to_all x4, blocking collectives: 50.4 us -> 49.4 us  [exchange(): lax.all_to_all(blocks, 'dp', 0, 0, axis_index_groups=LAYERS, tiled=True)]
where the time goes in v5:
time: 91 us; the launch traced here: 90.7 us
  blocking collectives  49.4 us (54%)
  starting transfers between devices  22.5 us (25%)
  Pallas kernels  11.8 us (13%)
  waiting for transfers between devices  5.68 us (6%)
    all_to_all x4, blocking collectives, exchange(): lax.all_to_all(blocks, 'dp', 0, 0, axis_index_groups=LAYERS, tiled=True)  49.4 us
    ppermute x6, starting transfers between devices, sum_over_replicas(): met.append(lax.ppermute(part, 'dp', partners))  13.5 us
    ppermute x1, starting transfers between devices, body(): received = lax.ppermute(other, 'tensor', PAIR)  4.88 us
    ppermute x6, waiting for transfers between devices, sum_over_replicas(): met.append(lax.ppermute(part, 'dp', partners))  4.67 us
    ppermute x1, starting transfers between devices, body(): other = lax.ppermute(own, 'tensor', PAIR)  4.11 us
    pallas_call x1, Pallas kernels, finish(): pl.pallas_call(kernel, in_specs=[pl.BlockSpec(memory_space=pltpu.SMEM), W...  4 us
    pallas_call x1, Pallas kernels, local_left(): pl.pallas_call(left_kernel, in_specs=[pl.BlockSpec(memory_space=pltpu.SME...  3.59 us
  transfers between devices with their start and end apart: 8, of which 4 were waited for; matrix products, arithmetic and copies ran while one was open for 0% of the time, Pallas kernels for 3%

profile of v5, /device:TPU:1, one launch (start us, length us, event | category | flops | bytes accessed | tf_op | source)
XLA Modules:
  0.0 90.7 jit_solution(7486596604960051574)
XLA Ops:
  0.6 3.6 %local_left.1 = (f32[32,1,1152]{2,1,0:T(1,128)S(1)}, f32[2,768,384]{2,1,0:T(8,128)S(1)}, f32[1,384,384]{2,1,0:T(8,128)S(1)}) custom-call(s32[1]{0:T(128)} %bitcast.core_ref.refs_0_, bf16[1,3,768,384]{3,2,1,0:T(8,128)(2,1)} %refs_2_.1, f32[1,3,768,384]{3,2,1,0:T(8,128)} %refs_3_.1, f32[3,32,768]{2,1,0:T(8,128)} %bitcast.3), custom_call_target="tpu_custom_call" | custom-call | tf_op jit(solution)/shard_map/left/local_left/pallas_call | solution.py:109
  4.2 16.5 %all_to_all.20 = f32[32,1,1152]{2,1,0:T(1,128)S(1)} all-to-all(f32[32,1,1152]{2,1,0:T(1,128)S(1)} %get-tuple-element.24), channel_id=1, replica_groups={{0,2,4,6,64,66,68,70,128,130,132,134,192,194,196,198,8,10,12,14,72,74,7..., dimensions={0} | all-to-all | bytes 294912 | tf_op jit(solution)/shard_map/sum_left/all_to_all | solution.py:409
  20.7 0.1 reduce_sum.22
  20.9 3.1 %collective-permute-start.1 = (f32[1,1152]{1,0:T(1,128)S(1)}, f32[1,1152]{1,0:T(1,128)S(1)}, u32[]{:S(2)}, u32[]{:S(2)}) collective-permute-start(f32[1,1152]{1,0:T(1,128)S(1)} %reduce_sum.23), channel_id=1, source_target_pairs={{0,24},{2,26},{4,28},{6,30},{8,48},{10,50},{12,52},{14,54},{16,40}... | collective-permute-start | bytes 13832 | tf_op jit(solution)/shard_map/sum_left/ppermute | solution.py:426
  23.9 4.7 %collective-permute-start.2 = (f32[1,1152]{1,0:T(1,128)S(1)}, f32[1,1152]{1,0:T(1,128)S(1)}, u32[]{:S(2)}, u32[]{:S(2)}) collective-permute-start(f32[1,1152]{1,0:T(1,128)S(1)} %reduce_sum.23), channel_id=1, source_target_pairs={{0,32},{2,34},{4,36},{6,38},{8,40},{10,42},{12,44},{14,46},{16,48}... | collective-permute-start | bytes 13832 | tf_op jit(solution)/shard_map/sum_left/ppermute | solution.py:426
  28.6 0.0 collective-permute-start
  28.6 0.0 collective-permute-done.1
  28.6 1.7 %collective-permute-done.2 = f32[1,1152]{1,0:T(1,128)S(1)} collective-permute-done((f32[1,1152]{1,0:T(1,128)S(1)}, f32[1,1152]{1,0:T(1,128)S(1)}, u32[]{:S(2)}, u32[]{:S(2)}) %collective-permute-start.2) | collective-permute-done | bytes 4640 | tf_op jit(solution)/shard_map/sum_left/ppermute | solution.py:426
  30.3 2.3 %collective-permute-done = f32[1,1152]{1,0:T(1,128)S(1)} collective-permute-done((f32[1,1152]{1,0:T(1,128)S(1)}, f32[1,1152]{1,0:T(1,128)S(1)}, u32[]{:S(2)}, u32[]{:S(2)}) %collective-permute-start) | collective-permute-done | bytes 4640 | tf_op jit(solution)/shard_map/sum_left/ppermute | solution.py:426
  32.6 0.1 broadcast_in_dim.21
  32.7 11.2 %all_to_all.21.left_ref.refs_4_ = f32[32,1,1152]{2,1,0:T(1,128)S(1)} all-to-all(f32[32,1,1152]{2,1,0:T(1,128)S(1)} %broadcast_in_dim.21), channel_id=1, replica_groups={{0,2,4,6,64,66,68,70,128,130,132,134,192,194,196,198,8,10,12,14,72,74,7..., dimensions={0} | all-to-all | bytes 294912 | tf_op jit(solution)/shard_map/sum_left/all_to_all | solution.py:409
  43.9 1.1 %right_other.1 = (f32[32,1,1536]{2,1,0:T(1,128)S(1)}, f32[32,1,384]{2,1,0:T(1,128)S(1)}) custom-call(s32[1]{0:T(128)} %bitcast.core_ref.refs_0_, f32[2,768,384]{2,1,0:T(8,128)S(1)} %get-tuple-element.23.kept_ref.refs_1_, f32[1,384,384]{2,1,0:T(8,128)S(1)} %get-tuple-element.25.half_ref, f32[32,1,1152]{2,1,0:T(1,128)S(1)} %all_to_all.21.left_ref.refs_4_), custom_call_target="tpu_custom_call" | custom-call | tf_op jit(solution)/shard_map/right/right_other/pallas_call | solution.py:173
  44.9 4.9 %collective-permute-start.3 = (f32[32,1,1536]{2,1,0:T(1,128)S(1)}, f32[32,1,1536]{2,1,0:T(1,128)S(1)}, u32[]{:S(2)}, u32[]{:S(2)}) collective-permute-start(f32[32,1,1536]{2,1,0:T(1,128)S(1)} %get-tuple-element.26), channel_id=1, source_target_pairs={{0,1},{1,0},{2,3},{3,2},{4,5},{5,4},{6,7},{7,6},{8,9},{9,8},{10,11... | collective-permute-start | bytes 589832 | tf_op jit(solution)/shard_map/right/ppermute | solution.py:446
  49.8 1.8 %right_own.1 = f32[32,1,1152]{2,1,0:T(1,128)S(1)} custom-call(s32[1]{0:T(128)} %bitcast.core_ref.refs_0_, f32[2,768,384]{2,1,0:T(8,128)S(1)} %get-tuple-element.23.kept_ref.refs_1_, bf16[1,3,768,384]{3,2,1,0:T(8,128)(2,1)} %refs_2_.1, f32[1,3,768,384]{3,2,1,0:T(8,128)} %refs_3_.1, f32[32,1,1152]{2,1,0:T(1,128)S(1)} %all_to_all.21.left_ref.refs_4_), custom_call_target="tpu_custom_call" | custom-call | flops 200000000 | bytes 2000000 | tf_op jit(solution)/shard_map/right/right_own/pallas_call | solution.py:187
  51.6 0.0 collective-permute-done.3
  51.6 0.1 slice_add_fusion.1.gram_ref
  51.7 0.2 slice_add_fusion
  51.8 10.8 %all_to_all.22 = f32[32,1,1152]{2,1,0:T(1,128)S(1)} all-to-all(f32[32,1,1152]{2,1,0:T(1,128)S(1)} %slice_add_fusion), channel_id=1, replica_groups={{0,2,4,6,64,66,68,70,128,130,132,134,192,194,196,198,8,10,12,14,72,74,7..., dimensions={0} | all-to-all | bytes 294912 | tf_op jit(solution)/shard_map/sum_right/all_to_all | solution.py:409
  62.6 0.1 reduce_sum.24
  62.7 2.2 %collective-permute-start.6 = (f32[1,1152]{1,0:T(1,128)S(1)}, f32[1,1152]{1,0:T(1,128)S(1)}, u32[]{:S(2)}, u32[]{:S(2)}) collective-permute-start(f32[1,1152]{1,0:T(1,128)S(1)} %reduce_sum.25), channel_id=1, source_target_pairs={{0,32},{2,34},{4,36},{6,38},{8,40},{10,42},{12,44},{14,46},{16,48}... | collective-permute-start | bytes 13832 | tf_op jit(solution)/shard_map/sum_right/ppermute | solution.py:426
  64.9 1.6 %collective-permute-start.5 = (f32[1,1152]{1,0:T(1,128)S(1)}, f32[1,1152]{1,0:T(1,128)S(1)}, u32[]{:S(2)}, u32[]{:S(2)}) collective-permute-start(f32[1,1152]{1,0:T(1,128)S(1)} %reduce_sum.25), channel_id=1, source_target_pairs={{0,24},{2,26},{4,28},{6,30},{8,48},{10,50},{12,52},{14,54},{16,40}... | collective-permute-start | bytes 13832 | tf_op jit(solution)/shard_map/sum_right/ppermute | solution.py:426
  66.5 1.9 %collective-permute-start.4 = (f32[1,1152]{1,0:T(1,128)S(1)}, f32[1,1152]{1,0:T(1,128)S(1)}, u32[]{:S(2)}, u32[]{:S(2)}) collective-permute-start(f32[1,1152]{1,0:T(1,128)S(1)} %reduce_sum.25), channel_id=1, source_target_pairs={{0,56},{2,58},{4,60},{6,62},{8,16},{10,18},{12,20},{14,22},{16,8},... | collective-permute-start | bytes 13832 | tf_op jit(solution)/shard_map/sum_right/ppermute | solution.py:426
  68.5 1.3 %inverse_factor.1.refs_7_ = f32[3,32,32]{2,1,0:T(8,128)S(1)} custom-call(f32[32,1,384]{2,1,0:T(1,128)S(1)} %slice_add_fusion.1.gram_ref), custom_call_target="tpu_custom_call" | custom-call | flops 4000000 | bytes 100000 | tf_op jit(solution)/shard_map/sum_right/inverse_factor/pallas_call | solution.py:256
  69.8 0.0 collective-permute-done.6
  69.8 0.0 collective-permute-done.5
  69.8 0.7 collective-permute-done.4
  70.5 0.1 broadcast_in_dim.23
  70.6 11.0 %all_to_all.23.refs_5_ = f32[32,1,1152]{2,1,0:T(1,128)S(1)} all-to-all(f32[32,1,1152]{2,1,0:T(1,128)S(1)} %broadcast_in_dim.23), channel_id=1, replica_groups={{0,2,4,6,64,66,68,70,128,130,132,134,192,194,196,198,8,10,12,14,72,74,7..., dimensions={0} | all-to-all | bytes 294912 | tf_op jit(solution)/shard_map/sum_right/all_to_all | solution.py:409
  81.6 4.1 %collective-permute-start.7 = (f32[32,1,1152]{2,1,0:T(1,128)S(1)}, f32[32,1,1152]{2,1,0:T(1,128)S(1)}, u32[]{:S(2)}, u32[]{:S(2)}) collective-permute-start(f32[32,1,1152]{2,1,0:T(1,128)S(1)} %all_to_all.23.refs_5_), channel_id=1, source_target_pairs={{0,1},{1,0},{2,3},{3,2},{4,5},{5,4},{6,7},{7,6},{8,9},{9,8},{10,11... | collective-permute-start | bytes 442376 | tf_op jit(solution)/shard_map/sum_right/ppermute | solution.py:453
  85.7 1.0 %collective-permute-done.7.refs_6_ = f32[32,1,1152]{2,1,0:T(1,128)S(1)} collective-permute-done((f32[32,1,1152]{2,1,0:T(1,128)S(1)}, f32[32,1,1152]{2,1,0:T(1,128)S(1)}, u32[]{:S(2)}, u32[]{:S(2)}) %collective-permute-start.7) | collective-permute-done | bytes 147488 | tf_op jit(solution)/shard_map/sum_right/ppermute | solution.py:453
  86.7 4.0 %finish.1 = (f32[1,3,768,384]{3,2,1,0:T(8,128)}, bf16[3,768,384]{2,1,0:T(8,128)(2,1)}, f32[3,32,768]{2,1,0:T(8,128)}) custom-call(s32[1]{0:T(128)} %bitcast.core_ref.refs_0_, f32[2,768,384]{2,1,0:T(8,128)S(1)} %get-tuple-element.23.kept_ref.refs_1_, bf16[1,3,768,384]{3,2,1,0:T(8,128)(2,1)} %refs_2_.1, f32[1,3,768,384]{3,2,1,0:T(8,128)} %refs_3_.1, ...), custom_call_target="tpu_custom_call" | custom-call | tf_op jit(solution)/shard_map/finish/finish/pallas_call | solution.py:364
  (4 shorter events, 0.1 us)
Async XLA Ops:
  20.9 7.7 %collective-permute-start.1 = (f32[1,1152]{1,0:T(1,128)S(1)}, f32[1,1152]{1,0:T(1,128)S(1)}, u32[]{:S(2)}, u32[]{:S(2)}) collective-permute-start(f32[1,1152]{1,0:T(1,128)S(1)} %reduce_sum.23), channel_id=1, source_target_pairs={{0,24},{2,26},{4,28},{6,30},{8,48},{10,50},{12,52},{14,54},{16,40}... | collective-permute-start | bytes 13832 | tf_op jit(solution)/shard_map/sum_left/ppermute | solution.py:426
  23.9 6.4 %collective-permute-start.2 = (f32[1,1152]{1,0:T(1,128)S(1)}, f32[1,1152]{1,0:T(1,128)S(1)}, u32[]{:S(2)}, u32[]{:S(2)}) collective-permute-start(f32[1,1152]{1,0:T(1,128)S(1)} %reduce_sum.23), channel_id=1, source_target_pairs={{0,32},{2,34},{4,36},{6,38},{8,40},{10,42},{12,44},{14,46},{16,48}... | collective-permute-start | bytes 13832 | tf_op jit(solution)/shard_map/sum_left/ppermute | solution.py:426
  28.6 4.0 %collective-permute-start = (f32[1,1152]{1,0:T(1,128)S(1)}, f32[1,1152]{1,0:T(1,128)S(1)}, u32[]{:S(2)}, u32[]{:S(2)}) collective-permute-start(f32[1,1152]{1,0:T(1,128)S(1)} %reduce_sum.23), channel_id=1, source_target_pairs={{0,56},{2,58},{4,60},{6,62},{8,16},{10,18},{12,20},{14,22},{16,8},... | collective-permute-start | bytes 13832 | tf_op jit(solution)/shard_map/sum_left/ppermute | solution.py:426
  44.9 6.7 %collective-permute-start.3 = (f32[32,1,1536]{2,1,0:T(1,128)S(1)}, f32[32,1,1536]{2,1,0:T(1,128)S(1)}, u32[]{:S(2)}, u32[]{:S(2)}) collective-permute-start(f32[32,1,1536]{2,1,0:T(1,128)S(1)} %get-tuple-element.26), channel_id=1, source_target_pairs={{0,1},{1,0},{2,3},{3,2},{4,5},{5,4},{6,7},{7,6},{8,9},{9,8},{10,11... | collective-permute-start | bytes 589832 | tf_op jit(solution)/shard_map/right/ppermute | solution.py:446
  62.7 7.1 %collective-permute-start.6 = (f32[1,1152]{1,0:T(1,128)S(1)}, f32[1,1152]{1,0:T(1,128)S(1)}, u32[]{:S(2)}, u32[]{:S(2)}) collective-permute-start(f32[1,1152]{1,0:T(1,128)S(1)} %reduce_sum.25), channel_id=1, source_target_pairs={{0,32},{2,34},{4,36},{6,38},{8,40},{10,42},{12,44},{14,46},{16,48}... | collective-permute-start | bytes 13832 | tf_op jit(solution)/shard_map/sum_right/ppermute | solution.py:426
  64.9 4.9 %collective-permute-start.5 = (f32[1,1152]{1,0:T(1,128)S(1)}, f32[1,1152]{1,0:T(1,128)S(1)}, u32[]{:S(2)}, u32[]{:S(2)}) collective-permute-start(f32[1,1152]{1,0:T(1,128)S(1)} %reduce_sum.25), channel_id=1, source_target_pairs={{0,24},{2,26},{4,28},{6,30},{8,48},{10,50},{12,52},{14,54},{16,40}... | collective-permute-start | bytes 13832 | tf_op jit(solution)/shard_map/sum_right/ppermute | solution.py:426
  66.5 4.0 %collective-permute-start.4 = (f32[1,1152]{1,0:T(1,128)S(1)}, f32[1,1152]{1,0:T(1,128)S(1)}, u32[]{:S(2)}, u32[]{:S(2)}) collective-permute-start(f32[1,1152]{1,0:T(1,128)S(1)} %reduce_sum.25), channel_id=1, source_target_pairs={{0,56},{2,58},{4,60},{6,62},{8,16},{10,18},{12,20},{14,22},{16,8},... | collective-permute-start | bytes 13832 | tf_op jit(solution)/shard_map/sum_right/ppermute | solution.py:426
  81.6 5.1 %collective-permute-start.7 = (f32[32,1,1152]{2,1,0:T(1,128)S(1)}, f32[32,1,1152]{2,1,0:T(1,128)S(1)}, u32[]{:S(2)}, u32[]{:S(2)}) collective-permute-start(f32[32,1,1152]{2,1,0:T(1,128)S(1)} %all_to_all.23.refs_5_), channel_id=1, source_target_pairs={{0,1},{1,0},{2,3},{3,2},{4,5},{5,4},{6,7},{7,6},{8,9},{9,8},{10,11... | collective-permute-start | bytes 442376 | tf_op jit(solution)/shard_map/sum_right/ppermute | solution.py:453

commit v6 on v5

--- a/solution.py
+++ b/solution.py
@@ -208,7 +208,7 @@
     )(core, kept, in_hbm(gradients), in_hbm(error_feedback), left)
 
 
-def inverse_kernel(gram_ref, inverse_ref):
+def inverse_kernel(gram_ref, left_ref, inverse_ref, bases_ref):
     group, blocks = 4, RANK // 8
     wide = (8, 2 * RANK)
     row = lax.broadcasted_iota(jnp.int32, (RANK, RANK), 0)
@@ -221,7 +221,7 @@
         tables.append([table[8 * b : 8 * b + 8] for b in range(blocks)])
         pivots.append([jnp.zeros(wide, jnp.float32)] * blocks)
     for j in range(0, RANK, group):
-        home, at = j // 8, j % 8
+        home, top = j // 8, j % 8
         live = range(home, blocks)
         for m in range(MATS):
             table = tables[m]
@@ -229,53 +229,66 @@
                 {b: jnp.broadcast_to(table[b][:, j + q : j + q + 1], wide) for b in live}
                 for q in range(group)
             ]
-            rows = [table[home][at + q : at + q + 1] for q in range(group)]
+            rows = [table[home][top + q : top + q + 1] for q in range(group)]
             for q in range(group):
-                pivot = columns[q][home][at + q : at + q + 1]
-                pivots[m][home] = jnp.where(below == at + q, pivot, pivots[m][home])
+                pivot = columns[q][home][top + q : top + q + 1]
+                pivots[m][home] = jnp.where(below == top + q, pivot, pivots[m][home])
                 over = 1.0 / pivot
                 scaled = rows[q] * over
                 factor = dict(columns[q])
-                factor[home] = jnp.where(below > at + q, factor[home], 0.0)
+                factor[home] = jnp.where(below > top + q, factor[home], 0.0)
                 for later in range(q + 1, group):
-                    ratio = columns[later][home][at + q : at + q + 1] * over
+                    ratio = columns[later][home][top + q : top + q + 1] * over
                     for b in live:
                         columns[later][b] = columns[later][b] - factor[b] * ratio
                     rows[later] = (
-                        rows[later] - factor[home][at + later : at + later + 1] * scaled
+                        rows[later] - factor[home][top + later : top + later + 1] * scaled
                     )
                 for b in live:
                     table[b] = table[b] - factor[b] * scaled
     for m in range(MATS):
         table = jnp.concatenate([block[:, RANK:] for block in tables[m]], axis=0)
         pivot = jnp.concatenate([block[:, RANK:] for block in pivots[m]], axis=0)
-        inverse_ref[m] = table * lax.rsqrt(pivot)
-
-
-def inverse_factor(gram):
+        inverse = table * lax.rsqrt(pivot)
+        inverse_ref[m] = inverse
+        basis = jnp.dot(
+            inverse,
+            left_ref[:, 0, at(m)],
+            precision=EXACT,
+            preferred_element_type=jnp.float32,
+        )
+        high, mid, _ = split(basis)
+        bases_ref[m] = jnp.concatenate([high, mid, high], axis=0)
+
+
+def inverse_factor(gram, left):
     return pl.pallas_call(
         inverse_kernel,
-        in_specs=[WHOLE],
-        out_specs=WHOLE,
-        out_shape=jax.ShapeDtypeStruct((MATS, RANK, RANK), jnp.float32),
+        in_specs=[WHOLE] * 2,
+        out_specs=[WHOLE] * 2,
+        out_shape=[
+            jax.ShapeDtypeStruct((MATS, RANK, RANK), jnp.float32),
+            jax.ShapeDtypeStruct((MATS, 3 * RANK, HALF), jnp.bfloat16),
+        ],
         compiler_params=PARAMS,
         cost_estimate=pl.CostEstimate(
             flops=4_000_000, bytes_accessed=100_000, transcendentals=0
         ),
         name="inverse_factor",
-    )(gram)
+    )(gram, left)
 
 
 def finish_kernel(
     replicas,
     core_ref,
     kept_ref,
+    half_ref,
     g_ref,
     e_ref,
-    left_ref,
     own_ref,
     other_ref,
     inverse_ref,
+    bases_ref,
     weights_ref,
     error_ref,
     new_ref,
@@ -294,8 +307,10 @@
     for m in range(MATS):
         pair = ()
         if m >= KEPT:
-            pair = fetches(
-                g_ref, e_ref, g_buf.at[m - KEPT], m_buf.at[m - KEPT], in_sems, m
+            rows = half_of(core_ref[0], True)
+            pair = (
+                pltpu.make_async_copy(g_ref.at[0, m, rows], g_buf.at[m - KEPT], in_sems.at[m, 0]),
+                pltpu.make_async_copy(e_ref.at[0, m, rows], m_buf.at[m - KEPT], in_sems.at[m, 1]),
             )
         loads.append(
             (pltpu.make_async_copy(weights_ref.at[m], w_buf.at[m], w_sems.at[m]), *pair)
@@ -319,44 +334,38 @@
         right = jnp.dot(
             inverse, total, precision=EXACT, preferred_element_type=jnp.float32
         ) * (1.0 / replicas)
-        basis = jnp.dot(
-            inverse,
-            left_ref[:, 0, at(m)],
-            precision=EXACT,
-            preferred_element_type=jnp.float32,
-        )
         r_buf[m] = right
-        store(r_buf.at[m], right_ref.at[m])
         high, mid, _ = split(right)
         rights = jnp.concatenate([high, high, mid], axis=0)
-        high, mid, _ = split(basis)
-        bases = jnp.concatenate([high, mid, high], axis=0)
-        for copy in loads[m]:
+        for copy in loads[m][1:]:
             copy.wait()
         for c in range(ROWS // CHUNK):
             rows = pl.ds(c * CHUNK, CHUNK)
             update = lax.dot_general(
                 rights[:, c * CHUNK : (c + 1) * CHUNK],
-                bases,
+                bases_ref[m],
                 (((0,), (0,)), ((), ())),
                 preferred_element_type=jnp.float32,
             )
             if m < KEPT:
                 merged = kept_ref[m, rows, :]
             else:
-                merged = g_buf[m - KEPT, rows, :].astype(jnp.float32)
-                merged = merged + m_buf[m - KEPT, rows, :]
+                fetched = g_buf[m - KEPT].astype(jnp.float32) + m_buf[m - KEPT]
+                merged = jnp.where(core_ref[0] == c, fetched, half_ref[m - KEPT])
             e_buf[m, rows, :] = merged - update
             store(e_buf.at[m, rows], error_ref.at[0, m, rows])
+            if c == 0:
+                loads[m][0].wait()
             weights = w_buf[m, rows, :].astype(jnp.float32)
             w_buf[m, rows, :] = (weights - 0.5 * update).astype(jnp.bfloat16)
             store(w_buf.at[m, rows], new_ref.at[m, rows])
+        store(r_buf.at[m], right_ref.at[m])
     for copy in stores:
         copy.wait()
 
 
 def finish(
-    core, kept, gradients, error_feedback, left, own, other, inverse, weights, replicas
+    core, kept, half, gradients, error_feedback, own, other, inverse, bases, weights, replicas
 ):
     def kernel(*refs):
         finish_kernel(replicas, *refs)
@@ -365,6 +374,7 @@
         kernel,
         in_specs=[
             pl.BlockSpec(memory_space=pltpu.SMEM),
+            WHOLE,
             WHOLE,
             ANYWHERE,
             ANYWHERE,
@@ -381,8 +391,8 @@
             pltpu.HBM((MATS, RANK, ROWS), jnp.float32),
         ],
         scratch_shapes=[
-            pltpu.VMEM((MATS - KEPT, ROWS, HALF), jnp.bfloat16),
-            pltpu.VMEM((MATS - KEPT, ROWS, HALF), jnp.float32),
+            pltpu.VMEM((MATS - KEPT, HALF, HALF), jnp.bfloat16),
+            pltpu.VMEM((MATS - KEPT, HALF, HALF), jnp.float32),
             pltpu.VMEM((MATS, ROWS, HALF), jnp.bfloat16),
             pltpu.VMEM((MATS, ROWS, HALF), jnp.float32),
             pltpu.VMEM((MATS, RANK, ROWS), jnp.float32),
@@ -395,12 +405,13 @@
     )(
         core,
         kept,
+        half,
         in_hbm(gradients),
         in_hbm(error_feedback),
-        left,
         own,
         other,
         inverse,
+        bases,
         in_hbm(weights),
     )
 
@@ -426,7 +437,7 @@
         met.append(lax.ppermute(part, "dp", partners))
     if beside is not None:
         result = work(value)
-        *met, result = lax.optimization_barrier((*met, result))
+        met, result = lax.optimization_barrier((met, result))
     total = (part + met[0]) + (met[1] + met[2])
     return exchange(jnp.broadcast_to(total[None], blocks.shape)), result
 
@@ -449,18 +460,19 @@
             (own + received[:, :, :WIDTH], gram + received[:, :, WIDTH:])
         )
     with jax.named_scope("sum_right"):
-        own, inverse = sum_over_replicas(own, (inverse_factor, gram))
+        own, (inverse, bases) = sum_over_replicas(own, (lambda pair: inverse_factor(*pair), (gram, left)))
         other = lax.ppermute(own, "tensor", PAIR)
     with jax.named_scope("finish"):
         next_error, new_weights, right_rows = finish(
             core,
             kept,
+            half,
             gradients,
             error_feedback,
-            left,
             own,
             other,
             inverse,
+            bases,
             weights,
             replicas,
         )

time: 91 us -> 90.9 us (level)
  transfers between devices with their start and end apart: 8 -> 8, of which waited for: 4 -> 4; matrix products, arithmetic and copies ran while one was open for 0% -> 0% of each run, Pallas kernels for 3% -> 4%
where the time goes in v6:
time: 90.9 us; the launch traced here: 90.7 us
  blocking collectives  49.4 us (54%)
  starting transfers between devices  22.5 us (25%)
  Pallas kernels  11.9 us (13%)
  waiting for transfers between devices  5.47 us (6%)
    all_to_all x4, blocking collectives, exchange(): lax.all_to_all(blocks, 'dp', 0, 0, axis_index_groups=LAYERS, tiled=True)  49.4 us
    ppermute x6, starting transfers between devices, sum_over_replicas(): met.append(lax.ppermute(part, 'dp', partners))  13.5 us
    ppermute x1, starting transfers between devices, body(): received = lax.ppermute(other, 'tensor', PAIR)  4.88 us
    ppermute x6, waiting for transfers between devices, sum_over_replicas(): met.append(lax.ppermute(part, 'dp', partners))  4.46 us
    ppermute x1, starting transfers between devices, body(): other = lax.ppermute(own, 'tensor', PAIR)  4.11 us
    pallas_call x1, Pallas kernels, finish(): pl.pallas_call(kernel, in_specs=[pl.BlockSpec(memory_space=pltpu.SMEM), W...  3.97 us
    pallas_call x1, Pallas kernels, local_left(): pl.pallas_call(left_kernel, in_specs=[pl.BlockSpec(memory_space=pltpu.SME...  3.59 us
  transfers between devices with their start and end apart: 8, of which 4 were waited for; matrix products, arithmetic and copies ran while one was open for 0% of the time, Pallas kernels for 4%

profile of v6, /device:TPU:1, one launch (start us, length us, event | category | flops | bytes accessed | tf_op | source)
XLA Modules:
  0.0 90.7 jit_solution(18188001678028496565)
XLA Ops:
  0.6 3.6 %local_left.1 = (f32[32,1,1152]{2,1,0:T(1,128)S(1)}, f32[2,768,384]{2,1,0:T(8,128)S(1)}, f32[1,384,384]{2,1,0:T(8,128)S(1)}) custom-call(s32[1]{0:T(128)} %bitcast.core_ref.refs_0_, bf16[1,3,768,384]{3,2,1,0:T(8,128)(2,1)} %refs_3_.1, f32[1,3,768,384]{3,2,1,0:T(8,128)} %refs_4_.1, f32[3,32,768]{2,1,0:T(8,128)} %bitcast.3), custom_call_target="tpu_custom_call" | custom-call | tf_op jit(solution)/shard_map/left/local_left/pallas_call | solution.py:109
  4.2 16.5 %all_to_all.20 = f32[32,1,1152]{2,1,0:T(1,128)S(1)} all-to-all(f32[32,1,1152]{2,1,0:T(1,128)S(1)} %get-tuple-element.29), channel_id=1, replica_groups={{0,2,4,6,64,66,68,70,128,130,132,134,192,194,196,198,8,10,12,14,72,74,7..., dimensions={0} | all-to-all | bytes 294912 | tf_op jit(solution)/shard_map/sum_left/all_to_all | solution.py:420
  20.7 0.1 reduce_sum.22
  20.9 3.1 %collective-permute-start.1 = (f32[1,1152]{1,0:T(1,128)S(1)}, f32[1,1152]{1,0:T(1,128)S(1)}, u32[]{:S(2)}, u32[]{:S(2)}) collective-permute-start(f32[1,1152]{1,0:T(1,128)S(1)} %reduce_sum.23), channel_id=1, source_target_pairs={{0,24},{2,26},{4,28},{6,30},{8,48},{10,50},{12,52},{14,54},{16,40}... | collective-permute-start | bytes 13832 | tf_op jit(solution)/shard_map/sum_left/ppermute | solution.py:437
  23.9 4.7 %collective-permute-start.2 = (f32[1,1152]{1,0:T(1,128)S(1)}, f32[1,1152]{1,0:T(1,128)S(1)}, u32[]{:S(2)}, u32[]{:S(2)}) collective-permute-start(f32[1,1152]{1,0:T(1,128)S(1)} %reduce_sum.23), channel_id=1, source_target_pairs={{0,32},{2,34},{4,36},{6,38},{8,40},{10,42},{12,44},{14,46},{16,48}... | collective-permute-start | bytes 13832 | tf_op jit(solution)/shard_map/sum_left/ppermute | solution.py:437
  28.6 0.0 collective-permute-start
  28.6 0.0 collective-permute-done.1
  28.6 1.7 %collective-permute-done.2 = f32[1,1152]{1,0:T(1,128)S(1)} collective-permute-done((f32[1,1152]{1,0:T(1,128)S(1)}, f32[1,1152]{1,0:T(1,128)S(1)}, u32[]{:S(2)}, u32[]{:S(2)}) %collective-permute-start.2) | collective-permute-done | bytes 4640 | tf_op jit(solution)/shard_map/sum_left/ppermute | solution.py:437
  30.3 2.3 %collective-permute-done = f32[1,1152]{1,0:T(1,128)S(1)} collective-permute-done((f32[1,1152]{1,0:T(1,128)S(1)}, f32[1,1152]{1,0:T(1,128)S(1)}, u32[]{:S(2)}, u32[]{:S(2)}) %collective-permute-start) | collective-permute-done | bytes 4640 | tf_op jit(solution)/shard_map/sum_left/ppermute | solution.py:437
  32.6 0.1 broadcast_in_dim.21
  32.7 11.2 %all_to_all.21.left_ref = f32[32,1,1152]{2,1,0:T(1,128)S(1)} all-to-all(f32[32,1,1152]{2,1,0:T(1,128)S(1)} %broadcast_in_dim.21), channel_id=1, replica_groups={{0,2,4,6,64,66,68,70,128,130,132,134,192,194,196,198,8,10,12,14,72,74,7..., dimensions={0} | all-to-all | bytes 294912 | tf_op jit(solution)/shard_map/sum_left/all_to_all | solution.py:420
  43.9 1.1 %right_other.1 = (f32[32,1,1536]{2,1,0:T(1,128)S(1)}, f32[32,1,384]{2,1,0:T(1,128)S(1)}) custom-call(s32[1]{0:T(128)} %bitcast.core_ref.refs_0_, f32[2,768,384]{2,1,0:T(8,128)S(1)} %get-tuple-element.27.kept_ref.refs_1_, f32[1,384,384]{2,1,0:T(8,128)S(1)} %get-tuple-element.28.half_ref.refs_2_, f32[32,1,1152]{2,1,0:T(1,128)S(1)} %all_to_all.21.left_ref), custom_call_target="tpu_custom_call" | custom-call | tf_op jit(solution)/shard_map/right/right_other/pallas_call | solution.py:173
  44.9 4.9 %collective-permute-start.3 = (f32[32,1,1536]{2,1,0:T(1,128)S(1)}, f32[32,1,1536]{2,1,0:T(1,128)S(1)}, u32[]{:S(2)}, u32[]{:S(2)}) collective-permute-start(f32[32,1,1536]{2,1,0:T(1,128)S(1)} %get-tuple-element.30), channel_id=1, source_target_pairs={{0,1},{1,0},{2,3},{3,2},{4,5},{5,4},{6,7},{7,6},{8,9},{9,8},{10,11... | collective-permute-start | bytes 589832 | tf_op jit(solution)/shard_map/right/ppermute | solution.py:457
  49.8 1.8 %right_own.1 = f32[32,1,1152]{2,1,0:T(1,128)S(1)} custom-call(s32[1]{0:T(128)} %bitcast.core_ref.refs_0_, f32[2,768,384]{2,1,0:T(8,128)S(1)} %get-tuple-element.27.kept_ref.refs_1_, bf16[1,3,768,384]{3,2,1,0:T(8,128)(2,1)} %refs_3_.1, f32[1,3,768,384]{3,2,1,0:T(8,128)} %refs_4_.1, f32[32,1,1152]{2,1,0:T(1,128)S(1)} %all_to_all.21.left_ref), custom_call_target="tpu_custom_call" | custom-call | flops 200000000 | bytes 2000000 | tf_op jit(solution)/shard_map/right/right_own/pallas_call | solution.py:187
  51.6 0.0 collective-permute-done.3
  51.6 0.1 slice_add_fusion.1.gram_ref
  51.7 0.2 slice_add_fusion
  51.8 10.8 %all_to_all.22 = f32[32,1,1152]{2,1,0:T(1,128)S(1)} all-to-all(f32[32,1,1152]{2,1,0:T(1,128)S(1)} %slice_add_fusion), channel_id=1, replica_groups={{0,2,4,6,64,66,68,70,128,130,132,134,192,194,196,198,8,10,12,14,72,74,7..., dimensions={0} | all-to-all | bytes 294912 | tf_op jit(solution)/shard_map/sum_right/all_to_all | solution.py:420
  62.6 0.1 reduce_sum.24
  62.7 2.2 %collective-permute-start.6 = (f32[1,1152]{1,0:T(1,128)S(1)}, f32[1,1152]{1,0:T(1,128)S(1)}, u32[]{:S(2)}, u32[]{:S(2)}) collective-permute-start(f32[1,1152]{1,0:T(1,128)S(1)} %reduce_sum.25), channel_id=1, source_target_pairs={{0,32},{2,34},{4,36},{6,38},{8,40},{10,42},{12,44},{14,46},{16,48}... | collective-permute-start | bytes 13832 | tf_op jit(solution)/shard_map/sum_right/ppermute | solution.py:437
  64.9 1.6 %collective-permute-start.5 = (f32[1,1152]{1,0:T(1,128)S(1)}, f32[1,1152]{1,0:T(1,128)S(1)}, u32[]{:S(2)}, u32[]{:S(2)}) collective-permute-start(f32[1,1152]{1,0:T(1,128)S(1)} %reduce_sum.25), channel_id=1, source_target_pairs={{0,24},{2,26},{4,28},{6,30},{8,48},{10,50},{12,52},{14,54},{16,40}... | collective-permute-start | bytes 13832 | tf_op jit(solution)/shard_map/sum_right/ppermute | solution.py:437
  66.5 1.9 %collective-permute-start.4 = (f32[1,1152]{1,0:T(1,128)S(1)}, f32[1,1152]{1,0:T(1,128)S(1)}, u32[]{:S(2)}, u32[]{:S(2)}) collective-permute-start(f32[1,1152]{1,0:T(1,128)S(1)} %reduce_sum.25), channel_id=1, source_target_pairs={{0,56},{2,58},{4,60},{6,62},{8,16},{10,18},{12,20},{14,22},{16,8},... | collective-permute-start | bytes 13832 | tf_op jit(solution)/shard_map/sum_right/ppermute | solution.py:437
  68.5 1.5 %inverse_factor.1 = (f32[3,32,32]{2,1,0:T(8,128)S(1)}, bf16[3,96,384]{2,1,0:T(8,128)(2,1)S(1)}) custom-call(f32[32,1,384]{2,1,0:T(1,128)S(1)} %slice_add_fusion.1.gram_ref, f32[32,1,1152]{2,1,0:T(1,128)S(1)} %all_to_all.21.left_ref), custom_call_target="tpu_custom_call" | custom-call | flops 4000000 | bytes 100000 | tf_op jit(solution)/shard_map/sum_right/inverse_factor/pallas_call | solution.py:265
  70.0 0.0 collective-permute-done.6
  70.0 0.0 collective-permute-done.5
  70.0 0.5 collective-permute-done.4
  70.5 0.1 broadcast_in_dim.23
  70.6 11.0 %all_to_all.23.refs_5_ = f32[32,1,1152]{2,1,0:T(1,128)S(1)} all-to-all(f32[32,1,1152]{2,1,0:T(1,128)S(1)} %broadcast_in_dim.23), channel_id=1, replica_groups={{0,2,4,6,64,66,68,70,128,130,132,134,192,194,196,198,8,10,12,14,72,74,7..., dimensions={0} | all-to-all | bytes 294912 | tf_op jit(solution)/shard_map/sum_right/all_to_all | solution.py:420
  81.6 4.1 %collective-permute-start.7 = (f32[32,1,1152]{2,1,0:T(1,128)S(1)}, f32[32,1,1152]{2,1,0:T(1,128)S(1)}, u32[]{:S(2)}, u32[]{:S(2)}) collective-permute-start(f32[32,1,1152]{2,1,0:T(1,128)S(1)} %all_to_all.23.refs_5_), channel_id=1, source_target_pairs={{0,1},{1,0},{2,3},{3,2},{4,5},{5,4},{6,7},{7,6},{8,9},{9,8},{10,11... | collective-permute-start | bytes 442376 | tf_op jit(solution)/shard_map/sum_right/ppermute | solution.py:464
  85.7 1.0 %collective-permute-done.7.refs_6_ = f32[32,1,1152]{2,1,0:T(1,128)S(1)} collective-permute-done((f32[32,1,1152]{2,1,0:T(1,128)S(1)}, f32[32,1,1152]{2,1,0:T(1,128)S(1)}, u32[]{:S(2)}, u32[]{:S(2)}) %collective-permute-start.7) | collective-permute-done | bytes 147488 | tf_op jit(solution)/shard_map/sum_right/ppermute | solution.py:464
  86.7 4.0 %finish.1 = (f32[1,3,768,384]{3,2,1,0:T(8,128)}, bf16[3,768,384]{2,1,0:T(8,128)(2,1)}, f32[3,32,768]{2,1,0:T(8,128)}) custom-call(s32[1]{0:T(128)} %bitcast.core_ref.refs_0_, f32[2,768,384]{2,1,0:T(8,128)S(1)} %get-tuple-element.27.kept_ref.refs_1_, f32[1,384,384]{2,1,0:T(8,128)S(1)} %get-tuple-element.28.half_ref.refs_2_, bf16[1,3,768,384]{3,2,1,0:T(8,128)(2,1)} %refs_3_.1, ...), custom_call_target="tpu_custom_call" | custom-call | tf_op jit(solution)/shard_map/finish/finish/pallas_call | solution.py:373
  (4 shorter events, 0.1 us)
Async XLA Ops:
  20.9 7.7 %collective-permute-start.1 = (f32[1,1152]{1,0:T(1,128)S(1)}, f32[1,1152]{1,0:T(1,128)S(1)}, u32[]{:S(2)}, u32[]{:S(2)}) collective-permute-start(f32[1,1152]{1,0:T(1,128)S(1)} %reduce_sum.23), channel_id=1, source_target_pairs={{0,24},{2,26},{4,28},{6,30},{8,48},{10,50},{12,52},{14,54},{16,40}... | collective-permute-start | bytes 13832 | tf_op jit(solution)/shard_map/sum_left/ppermute | solution.py:437
  23.9 6.4 %collective-permute-start.2 = (f32[1,1152]{1,0:T(1,128)S(1)}, f32[1,1152]{1,0:T(1,128)S(1)}, u32[]{:S(2)}, u32[]{:S(2)}) collective-permute-start(f32[1,1152]{1,0:T(1,128)S(1)} %reduce_sum.23), channel_id=1, source_target_pairs={{0,32},{2,34},{4,36},{6,38},{8,40},{10,42},{12,44},{14,46},{16,48}... | collective-permute-start | bytes 13832 | tf_op jit(solution)/shard_map/sum_left/ppermute | solution.py:437
  28.6 4.0 %collective-permute-start = (f32[1,1152]{1,0:T(1,128)S(1)}, f32[1,1152]{1,0:T(1,128)S(1)}, u32[]{:S(2)}, u32[]{:S(2)}) collective-permute-start(f32[1,1152]{1,0:T(1,128)S(1)} %reduce_sum.23), channel_id=1, source_target_pairs={{0,56},{2,58},{4,60},{6,62},{8,16},{10,18},{12,20},{14,22},{16,8},... | collective-permute-start | bytes 13832 | tf_op jit(solution)/shard_map/sum_left/ppermute | solution.py:437
  44.9 6.7 %collective-permute-start.3 = (f32[32,1,1536]{2,1,0:T(1,128)S(1)}, f32[32,1,1536]{2,1,0:T(1,128)S(1)}, u32[]{:S(2)}, u32[]{:S(2)}) collective-permute-start(f32[32,1,1536]{2,1,0:T(1,128)S(1)} %get-tuple-element.30), channel_id=1, source_target_pairs={{0,1},{1,0},{2,3},{3,2},{4,5},{5,4},{6,7},{7,6},{8,9},{9,8},{10,11... | collective-permute-start | bytes 589832 | tf_op jit(solution)/shard_map/right/ppermute | solution.py:457
  62.7 7.3 %collective-permute-start.6 = (f32[1,1152]{1,0:T(1,128)S(1)}, f32[1,1152]{1,0:T(1,128)S(1)}, u32[]{:S(2)}, u32[]{:S(2)}) collective-permute-start(f32[1,1152]{1,0:T(1,128)S(1)} %reduce_sum.25), channel_id=1, source_target_pairs={{0,32},{2,34},{4,36},{6,38},{8,40},{10,42},{12,44},{14,46},{16,48}... | collective-permute-start | bytes 13832 | tf_op jit(solution)/shard_map/sum_right/ppermute | solution.py:437
  64.9 5.1 %collective-permute-start.5 = (f32[1,1152]{1,0:T(1,128)S(1)}, f32[1,1152]{1,0:T(1,128)S(1)}, u32[]{:S(2)}, u32[]{:S(2)}) collective-permute-start(f32[1,1152]{1,0:T(1,128)S(1)} %reduce_sum.25), channel_id=1, source_target_pairs={{0,24},{2,26},{4,28},{6,30},{8,48},{10,50},{12,52},{14,54},{16,40}... | collective-permute-start | bytes 13832 | tf_op jit(solution)/shard_map/sum_right/ppermute | solution.py:437
  66.5 4.0 %collective-permute-start.4 = (f32[1,1152]{1,0:T(1,128)S(1)}, f32[1,1152]{1,0:T(1,128)S(1)}, u32[]{:S(2)}, u32[]{:S(2)}) collective-permute-start(f32[1,1152]{1,0:T(1,128)S(1)} %reduce_sum.25), channel_id=1, source_target_pairs={{0,56},{2,58},{4,60},{6,62},{8,16},{10,18},{12,20},{14,22},{16,8},... | collective-permute-start | bytes 13832 | tf_op jit(solution)/shard_map/sum_right/ppermute | solution.py:437
  81.6 5.1 %collective-permute-start.7 = (f32[32,1,1152]{2,1,0:T(1,128)S(1)}, f32[32,1,1152]{2,1,0:T(1,128)S(1)}, u32[]{:S(2)}, u32[]{:S(2)}) collective-permute-start(f32[32,1,1152]{2,1,0:T(1,128)S(1)} %all_to_all.23.refs_5_), channel_id=1, source_target_pairs={{0,1},{1,0},{2,3},{3,2},{4,5},{5,4},{6,7},{7,6},{8,9},{9,8},{10,11... | collective-permute-start | bytes 442376 | tf_op jit(solution)/shard_map/sum_right/ppermute | solution.py:464
